TPU v7x, 256 devices: a whole 4x4x8 slice. The times are simulated.
256 devices in a mesh: macro: 16 (over x, y), tile: 8 (over z), micro: 2 (over core).
Axes of the slice: x: 4, y: 4, z: 8, core: 2. Of those that a mesh axis runs over, the one named last changes fastest.
Arguments:
- velocity: float32 [3, 384, 64, 256], P(None, 'macro', 'tile', 'micro'), may hold values from -6 to 6
- viscosity: float32 [384, 64, 256], P('macro', 'tile', 'micro'), may hold values from 0.3 to 3
- flag_cell: int32 [8192], P(('macro', 'tile', 'micro')), may hold values from 1153 to 23422, as said below
- flag_owner: int32 [8192, 1], P(('macro', 'tile', 'micro')), may hold values from 0 to 31; in each aligned block of 32 rows (0 to 31, 32 to 63, ...) at most 2 rows name the same one
- conformations: float32 [3, 16384, 512], P(None, ('macro', 'tile', 'micro')), may hold values from -3.2 to 3.2
- increments: bfloat16 [16, 3, 16384, 512], P(None, None, ('macro', 'tile', 'micro')), may hold values from -4 to 4
Outputs:
- velocity_next: float32 [3, 384, 64, 256], P(None, 'macro', 'tile', 'micro')
- conformations_next: float32 [3, 16384, 512], P(None, ('macro', 'tile', 'micro'))
- flag_stress: float32 [6, 8192], P(None, ('macro', 'tile', 'micro'))
Inputs may be any that keep to these rules, and one draw needn't show every extreme that they name: `flag_cell`: on each device 32 distinct cells of its own block, none of them on a face of the block. `flag_owner`: among the 32 entries of one device at most 2 name the same owner, and some device has an owner named 2 times.
All inputs are finite; a program needn't handle non-finite values.
Results may differ from a plain program's by a relative error of at most 0.0003.
Values sent between devices are 32-bit elements; how exact they have to be, the bound alone decides.
A program may use at most 64 MiB of HBM per device.

v0:
```python
import jax
import jax.numpy as jnp
from jax import lax
from jax.sharding import PartitionSpec as P

stress_pairs = ((0, 0), (1, 1), (2, 2), (0, 1), (0, 2), (1, 2))
macro_step = 0.1
micro_step = 0.01
noise_weight = 0.1
relax_rate = 0.5
fene_extent = 30.0
spring_floor = 0.1
polymer_weight = 0.25


def padded_2(block, sides, width):
    for axis, dim in sides:
        count = lax.axis_size(axis)
        forward = [(i, i + 1) for i in range(count - 1)]
        backward = [(target, source) for source, target in forward]
        low = lax.ppermute(
            lax.slice_in_dim(block, block.shape[dim] - width, None, axis=dim), axis, forward
        )
        high = lax.ppermute(lax.slice_in_dim(block, 0, width, axis=dim), axis, backward)
        block = jnp.concatenate([low, block, high], axis=dim)
    return block


def pair_index(left_axis, right_axis):
    return stress_pairs.index((min(left_axis, right_axis), max(left_axis, right_axis)))


def window(source, direction, offset):
    slicers = [slice(None)]
    for spatial in range(3):
        length = source.shape[spatial + 1] - 2
        if spatial == direction:
            slicers.append(slice(offset, offset + length))
        else:
            slicers.append(slice(1, 1 + length))
    return source[tuple(slicers)]


def stress_field(padded, viscous):
    slopes = [
        (window(padded, direction, 2) - window(padded, direction, 0)) * 0.5
        for direction in range(3)
    ]
    components = [
        viscous * (slopes[right_axis][left_axis] + slopes[left_axis][right_axis])
        for left_axis, right_axis in stress_pairs
    ]
    return jnp.stack(components, axis=0)


def divergence(padded_stress):
    result = []
    for left_axis in range(3):
        summed = None
        for right_axis in range(3):
            member = pair_index(left_axis, right_axis)
            column = padded_stress[member : member + 1]
            change = (window(column, right_axis, 2) - window(column, right_axis, 0))[0] * 0.5
            summed = change if summed is None else summed + change
        result.append(summed)
    return jnp.stack(result, axis=0)


def spring_of(current):
    return 1.0 / jnp.maximum(
        1.0
        - (current[0] * current[0] + current[1] * current[1] + current[2] * current[2])
        / fene_extent,
        spring_floor,
    )


def advance(conform, gradient_in, noise):
    rate_table = gradient_in[:, :, None]

    def substep(substep_index, current):
        spring = spring_of(current)
        updated = []
        for left_axis in range(3):
            drift_term = (
                rate_table[3 * left_axis] * current[0]
                + rate_table[3 * left_axis + 1] * current[1]
                + rate_table[3 * left_axis + 2] * current[2]
                - relax_rate * spring * current[left_axis]
            )
            updated.append(
                current[left_axis]
                + micro_step * drift_term
                + noise_weight * noise[substep_index, left_axis].astype(jnp.float32)
            )
        return jnp.stack(updated, axis=0)

    last_state = lax.fori_loop(0, noise.shape[0], substep, conform)
    spring = spring_of(last_state)
    stresses = []
    for left_axis, right_axis in stress_pairs:
        identity_part = 1.0 if left_axis == right_axis else 0.0
        stresses.append(
            polymer_weight
            * (
                jnp.mean(spring * last_state[left_axis] * last_state[right_axis], axis=-1)
                - identity_part
            )
        )
    return (last_state, jnp.stack(stresses, axis=0))


def add_polymer(velocity_next, polymer_rows, flag_cell, strides):
    flattened = velocity_next.reshape(3, -1)
    index_parts = []
    value_parts = [[], [], []]
    for right_axis, stride in enumerate(strides):
        index_parts.append(flag_cell - stride)
        index_parts.append(flag_cell + stride)
        for left_axis in range(3):
            contribution = macro_step * 0.5 * polymer_rows[pair_index(left_axis, right_axis)]
            value_parts[left_axis].append(contribution)
            value_parts[left_axis].append(-contribution)
    targets = jnp.concatenate(index_parts, axis=0)
    updates = jnp.stack([jnp.concatenate(parts, axis=0) for parts in value_parts], axis=0)
    flattened = flattened.at[:, targets].add(updates)
    return flattened.reshape(velocity_next.shape)


def shards(velocity, viscosity, flag_cell, flag_owner, conformations, increments):
    macro_count = lax.axis_size("macro")
    micro_count = lax.axis_size("micro")
    owner_count = macro_count * micro_count
    slot_count = conformations.shape[1]
    capacity = slot_count // owner_count
    size_x, size_y, size_z = viscosity.shape
    strides = (size_y * size_z, size_z, 1)
    flat_velocity = velocity.reshape(3, size_x * size_y * size_z)
    slopes = []
    for stride in strides:
        upper_side = jnp.take(flat_velocity, flag_cell + stride, axis=1)
        lower_side = jnp.take(flat_velocity, flag_cell - stride, axis=1)
        slopes.append((upper_side - lower_side) * 0.5)
    gradient_rows = jnp.stack(slopes, axis=1).reshape(9, flag_cell.shape[0])
    viscous_flag = jnp.take(viscosity.reshape(-1), flag_cell)
    viscous_rows = jnp.stack(
        [
            viscous_flag
            * (
                gradient_rows[3 * left_axis + right_axis]
                + gradient_rows[3 * right_axis + left_axis]
            )
            for left_axis, right_axis in stress_pairs
        ],
        axis=0,
    )
    owner_index = flag_owner[:, 0]
    onehot = (owner_index[:, None] == jnp.arange(owner_count, dtype=jnp.int32)[None, :]).astype(
        jnp.int32
    )
    slot_rank = jnp.sum((jnp.cumsum(onehot, axis=0) - onehot) * onehot, axis=1)
    position = owner_index * capacity + slot_rank
    placing = (position[:, None] == jnp.arange(slot_count, dtype=jnp.int32)[None, :]).astype(
        jnp.float32
    )
    outgoing = jnp.dot(gradient_rows, placing, precision=lax.Precision.HIGHEST)
    gradient_in = lax.all_to_all(
        outgoing, ("macro", "micro"), split_axis=1, concat_axis=1, tiled=True
    )
    last_state, polymer = advance(conformations, gradient_in, increments)
    returned_rows = lax.all_to_all(
        polymer, ("macro", "micro"), split_axis=1, concat_axis=1, tiled=True
    )
    polymer_rows = jnp.dot(returned_rows, placing.T, precision=lax.Precision.HIGHEST)
    flag_stress = viscous_rows + polymer_rows
    padded = padded_2(velocity, (("macro", 1), ("tile", 2), ("micro", 3)), 1)
    stress_all = stress_field(padded, viscosity)
    stress_pad = padded_2(stress_all, (("macro", 1), ("tile", 2), ("micro", 3)), 1)
    velocity_next = velocity + macro_step * divergence(stress_pad)
    velocity_next = add_polymer(velocity_next, polymer_rows, flag_cell, strides)
    return (velocity_next, last_state, flag_stress)


def solution(mesh):
    in_specs = (
        P(None, "macro", "tile", "micro"),
        P("macro", "tile", "micro"),
        P(("macro", "tile", "micro")),
        P(("macro", "tile", "micro"), None),
        P(None, ("macro", "tile", "micro"), None),
        P(None, None, ("macro", "tile", "micro"), None),
    )
    out_specs = (
        P(None, "macro", "tile", "micro"),
        P(None, ("macro", "tile", "micro"), None),
        P(None, ("macro", "tile", "micro")),
    )
    return jax.shard_map(shards, mesh=mesh, in_specs=in_specs, out_specs=out_specs, check_vma=False)
```

profile of v0, /device:TPU:120, one launch (start us, length us, event | category | flops | bytes accessed | tf_op | source)
XLA Modules:
  0.0 226.0 jit_solution(9494538232161310312)
XLA Ops:
  1.4 3.0 %collective-permute-start.1 = (f32[3,1,8,128]{3,2,1,0:T(8,128)S(1)}, f32[3,1,8,128]{3,2,1,0:T(8,128)S(1)}, u32[]{:S(2)}, u32[]{:S(2)}) collective-permute-start(f32[3,1,8,128]{3,2,1,0:T(8,128)S(1)} %get-tuple-element.190), channel_id=1, source_target_pairs={{0,16},{16,32},{32,48},{48,64},{64,80},{80,96},{96,112},{112,128},... | collective-permute-start | bytes 36872 | tf_op jit(solution)/shard_map/ppermute | solution.py:21
  4.4 2.8 %collective-permute-start = (f32[3,1,8,128]{3,2,1,0:T(8,128)S(1)}, f32[3,1,8,128]{3,2,1,0:T(8,128)S(1)}, u32[]{:S(2)}, u32[]{:S(2)}) collective-permute-start(f32[3,1,8,128]{3,2,1,0:T(8,128)S(1)} %get-tuple-element.191), channel_id=1, source_target_pairs={{16,0},{32,16},{48,32},{64,48},{80,64},{96,80},{112,96},{128,112},... | collective-permute-start | bytes 36872 | tf_op jit(solution)/shard_map/ppermute | solution.py:24
  7.3 7.6 %copy.189 = f32[3,24,8,128]{0,3,2,1:T(8,128)} copy(f32[3,24,8,128]{3,2,1,0:T(8,128)} %param.10) | data formatting | bytes 589824 | tf_op args[0]
  15.2 5.1 %gather_fusion.6 = f32[32,3]{1,0:T(8,128)S(1)} fusion(f32[3,24576]{0,1:T(8,128)} %bitcast.224, s32[1024]{0:T(1024)S(1)} %get-tuple-element.228), kind=kCustom, calls=%fused_computation.5.clone | custom fusion | bytes 896 | tf_op jit(solution)/shard_map/jit(_take)/gather | solution.py:142
  20.5 5.2 %gather_fusion.5 = f32[32,3]{1,0:T(8,128)S(1)} fusion(f32[3,24576]{0,1:T(8,128)} %bitcast.225, s32[1024]{0:T(1024)S(1)} %get-tuple-element.229), kind=kCustom, calls=%fused_computation.4.clone | custom fusion | bytes 896 | tf_op jit(solution)/shard_map/jit(_take)/gather | solution.py:141
  25.7 5.2 %gather_fusion.4 = f32[32,3]{1,0:T(8,128)S(1)} fusion(f32[3,24576]{0,1:T(8,128)} %bitcast.226, s32[1024]{0:T(1024)S(1)} %get-tuple-element.230), kind=kCustom, calls=%fused_computation.3.clone | custom fusion | bytes 896 | tf_op jit(solution)/shard_map/jit(_take)/gather | solution.py:142
  30.9 5.2 %gather_fusion.3 = f32[32,3]{1,0:T(8,128)S(1)} fusion(f32[3,24576]{0,1:T(8,128)} %bitcast.227, s32[1024]{0:T(1024)S(1)} %get-tuple-element.231), kind=kCustom, calls=%fused_computation.2.clone | custom fusion | bytes 896 | tf_op jit(solution)/shard_map/jit(_take)/gather | solution.py:141
  36.2 5.2 %gather_fusion.2 = f32[32,3]{1,0:T(8,128)S(1)} fusion(f32[3,24576]{0,1:T(8,128)} %bitcast.228, s32[1024]{0:T(1024)S(1)} %get-tuple-element.232), kind=kCustom, calls=%fused_computation.1.clone | custom fusion | bytes 896 | tf_op jit(solution)/shard_map/jit(_take)/gather | solution.py:142
  41.3 5.1 %gather_fusion.1 = f32[32,3]{1,0:T(8,128)S(1)} fusion(f32[3,24576]{0,1:T(8,128)} %bitcast.229, s32[1024]{0:T(1024)S(1)} %get-tuple-element.233), kind=kCustom, calls=%fused_computation.clone | custom fusion | bytes 896 | tf_op jit(solution)/shard_map/jit(_take)/gather | solution.py:141
  47.7 7.3 %all-to-all-start = ((f32[9,32,2]{0,2,1:T(2,128)}), f32[9,32,2]{0,2,1:T(2,128)S(1)}, u32[]{:S(2)}, u32[]{:S(2)}) async-start(f32[9,32,2]{0,2,1:T(2,128)} %copy.197), calls=%async_computation | async-start | bytes 65536 | tf_op jit(solution)/shard_map/all_to_all | solution.py:167
  55.9 4.7 %all-to-all-done = f32[9,32,2]{0,2,1:T(2,128)S(1)} async-done(((f32[9,32,2]{0,2,1:T(2,128)}), f32[9,32,2]{0,2,1:T(2,128)S(1)}, u32[]{:S(2)}, u32[]{:S(2)}) %all-to-all-start) | async-done | bytes 2336 | tf_op jit(solution)/shard_map/all_to_all | solution.py:167
  60.7 33.2 %while.13 = (s32[]{:T(128)}, f32[3,64,512]{2,1,0:T(8,128)S(1)}, f32[9,64,1]{1,2,0:T(1,128)S(1)}, bf16[16,3,64,512]{3,2,1,0:T(8,128)(2,1)}, s32[]{:T(128)}) while((s32[]{:T(128)}, f32[3,64,512]{2,1,0:T(8,128)S(1)}, f32[9,64,1]{1,2,0:T(1,128)S(1)}, bf16[16,3,64,512]{3,2,1,0:T(8,128)(2,1)}, s32[]{:T(128)}) %tuple.126), condition=%wide.region_3.5_spmd, body=%wide.region_2.4_spmd.sunk | while | flops 2031618 | bytes 2169677 | solution.py:98
  95.9 5.6 %all-to-all-start.1 = ((f32[6,32,2]{0,2,1:T(2,128)}), f32[6,32,2]{0,2,1:T(2,128)S(1)}, u32[]{:S(2)}, u32[]{:S(2)}) async-start(f32[6,32,2]{0,2,1:T(2,128)} %copy.199), calls=%async_computation.1 | async-start | bytes 65536 | tf_op jit(solution)/shard_map/all_to_all | solution.py:171
  103.1 4.1 %all-to-all-done.1 = f32[6,32,2]{0,2,1:T(2,128)S(1)} async-done(((f32[6,32,2]{0,2,1:T(2,128)}), f32[6,32,2]{0,2,1:T(2,128)S(1)}, u32[]{:S(2)}, u32[]{:S(2)}) %all-to-all-start.1) | async-done | bytes 1568 | tf_op jit(solution)/shard_map/all_to_all | solution.py:171
  109.9 2.0 collective-permute-start.2
  112.0 5.0 %collective-permute-start.3 = (f32[3,26,1,128]{1,3,2,0:T(8,128)}, f32[3,26,1,128]{1,3,2,0:T(8,128)}, u32[]{:S(2)}, u32[]{:S(2)}) collective-permute-start(f32[3,26,1,128]{1,3,2,0:T(8,128)} %get-tuple-element.176), channel_id=1, source_target_pairs={{0,2},{2,4},{4,6},{6,8},{8,10},{10,12},{12,14},{1,3},{3,5},{5,7},{... | collective-permute-start | bytes 119816 | tf_op jit(solution)/shard_map/ppermute | solution.py:21
  117.8 1.4 copy.203
  119.2 1.7 copy.202
  122.4 1.3 collective-permute-start.4
  123.7 3.0 %collective-permute-start.5 = (f32[3,26,10,1]{1,3,2,0:T(1,128)S(1)}, f32[3,26,10,1]{1,3,2,0:T(1,128)S(1)}, u32[]{:S(2)}, u32[]{:S(2)}) collective-permute-start(f32[3,26,10,1]{1,3,2,0:T(1,128)S(1)} %get-tuple-element.174), channel_id=1, source_target_pairs={{0,1},{2,3},{4,5},{6,7},{8,9},{10,11},{12,13},{14,15},{16,17},{18,... | collective-permute-start | bytes 9368 | tf_op jit(solution)/shard_map/ppermute | solution.py:21
  127.6 2.8 %fusion.1 = (f32[3,24,8,128]{1,3,2,0:T(8,128)S(1)}, f32[3,24,8,128]{1,3,2,0:T(8,128)S(1)}) fusion(f32[3,26,10,1]{1,3,2,0:T(1,128)S(1)} %collective-permute-done.5, f32[3,26,1,128]{1,3,2,0:T(8,128)} %collective-permute-done.2, f32[3,26,8,128]{1,3,2,0:T(8,128)S(1)} %copy.159, f32[3,26,1,128]{1,3,2,0:T(8,128)} %collective-permute-done.3, ...), kind=kLoop, calls=%fused_computation.24 | loop fusion | flops 884736 | bytes 995424 | tf_op jit(solution)/shard_map/mul | solution.py:46
  132.1 4.0 %collective-permute-start.7 = (f32[6,1,8,128]{3,2,1,0:T(8,128)S(1)}, f32[6,1,8,128]{3,2,1,0:T(8,128)S(1)}, u32[]{:S(2)}, u32[]{:S(2)}) collective-permute-start(f32[6,1,8,128]{3,2,1,0:T(8,128)S(1)} %get-tuple-element.186), channel_id=1, source_target_pairs={{0,16},{16,32},{32,48},{48,64},{64,80},{80,96},{96,112},{112,128},... | collective-permute-start | bytes 73736 | tf_op jit(solution)/shard_map/ppermute | solution.py:21
  136.1 1.9 collective-permute-start.6
  139.5 4.5 %collective-permute-done.6 = f32[6,1,8,128]{3,2,1,0:T(8,128)S(1)} collective-permute-done((f32[6,1,8,128]{3,2,1,0:T(8,128)S(1)}, f32[6,1,8,128]{3,2,1,0:T(8,128)S(1)}, u32[]{:S(2)}, u32[]{:S(2)}) %collective-permute-start.6) | collective-permute-done | bytes 24608 | tf_op jit(solution)/shard_map/ppermute | solution.py:24
  145.4 2.0 copy.177
  148.4 5.6 %collective-permute-start.9 = (f32[6,26,1,128]{1,3,2,0:T(8,128)}, f32[6,26,1,128]{1,3,2,0:T(8,128)S(1)}, u32[]{:S(2)}, u32[]{:S(2)}) collective-permute-start(f32[6,26,1,128]{1,3,2,0:T(8,128)} %get-tuple-element.163), channel_id=1, source_target_pairs={{0,2},{2,4},{4,6},{6,8},{8,10},{10,12},{12,14},{1,3},{3,5},{5,7},{... | collective-permute-start | bytes 239624 | tf_op jit(solution)/shard_map/ppermute | solution.py:21
  154.0 1.9 collective-permute-start.8
  156.7 5.0 %collective-permute-done.9 = f32[6,26,1,128]{1,3,2,0:T(8,128)S(1)} collective-permute-done((f32[6,26,1,128]{1,3,2,0:T(8,128)}, f32[6,26,1,128]{1,3,2,0:T(8,128)S(1)}, u32[]{:S(2)}, u32[]{:S(2)}) %collective-permute-start.9) | collective-permute-done | bytes 79904 | tf_op jit(solution)/shard_map/ppermute | solution.py:21
  161.7 5.3 %collective-permute-done.8 = f32[6,26,1,128]{1,3,2,0:T(8,128)} collective-permute-done((f32[6,26,1,128]{1,3,2,0:T(8,128)}, f32[6,26,1,128]{1,3,2,0:T(8,128)}, u32[]{:S(2)}, u32[]{:S(2)}) %collective-permute-start.8) | collective-permute-done | bytes 79904 | tf_op jit(solution)/shard_map/ppermute | solution.py:24
  167.1 1.4 pad_maximum_fusion.29
  168.5 1.3 collective-permute-start.10
  169.8 4.2 %collective-permute-start.11 = (f32[6,26,10,1]{1,3,2,0:T(1,128)}, f32[6,26,10,1]{1,3,2,0:T(1,128)}, u32[]{:S(2)}, u32[]{:S(2)}) collective-permute-start(f32[6,26,10,1]{1,3,2,0:T(1,128)} %get-tuple-element.162), channel_id=1, source_target_pairs={{0,1},{2,3},{4,5},{6,7},{8,9},{10,11},{12,13},{14,15},{16,17},{18,... | collective-permute-start | bytes 18728 | tf_op jit(solution)/shard_map/ppermute | solution.py:21
  174.8 1.9 copy.205
  176.7 1.9 copy.207
  178.6 1.9 copy.209
  180.5 1.9 copy.208
  182.4 1.9 copy.206
  184.3 1.9 copy.204
  186.2 2.7 %fusion.6 = f32[1,24,8,128]{1,3,2,0:T(8,128)} fusion(f32[6,26,10,1]{1,3,2,0:T(1,128)} %collective-permute-done.11, f32[6,26,1,128]{1,3,2,0:T(8,128)} %collective-permute-done.8, f32[6,26,8,128]{1,3,2,0:T(8,128)S(1)} %copy.177, f32[6,26,1,128]{1,3,2,0:T(8,128)S(1)} %collective-permute-done.9, f32[6,26,10,1]{1,3,2,0:T(1,128)} %collective-permute-done.10, ...), kind=kLoop, calls=%fused_computation.39 | loop fusion | flops 344064 | bytes 1106112 | tf_op jit(solution)/shard_map/add | solution.py:64
  188.9 1.9 copy.187
  190.7 2.7 %fusion.13 = f32[1,24,8,128]{1,3,2,0:T(8,128)} fusion(f32[6,26,10,1]{1,3,2,0:T(1,128)} %collective-permute-done.11, f32[6,26,1,128]{1,3,2,0:T(8,128)} %collective-permute-done.8, f32[6,26,8,128]{1,3,2,0:T(8,128)S(1)} %copy.177, f32[6,26,1,128]{1,3,2,0:T(8,128)S(1)} %collective-permute-done.9, f32[6,26,10,1]{1,3,2,0:T(1,128)} %collective-permute-done.10, ...), kind=kLoop, calls=%fused_computation.56 | loop fusion | flops 344064 | bytes 1106112 | tf_op jit(solution)/shard_map/add | solution.py:64
  193.4 1.8 copy.185
  195.2 2.7 %fusion.10 = f32[1,24,8,128]{1,3,2,0:T(8,128)} fusion(f32[6,26,10,1]{1,3,2,0:T(1,128)} %collective-permute-done.11, f32[6,26,1,128]{1,3,2,0:T(8,128)} %collective-permute-done.8, f32[6,26,8,128]{1,3,2,0:T(8,128)S(1)} %copy.177, f32[6,26,1,128]{1,3,2,0:T(8,128)S(1)} %collective-permute-done.9, f32[6,26,10,1]{1,3,2,0:T(1,128)} %collective-permute-done.10, ...), kind=kLoop, calls=%fused_computation.51 | loop fusion | flops 344064 | bytes 1106112 | tf_op jit(solution)/shard_map/add | solution.py:64
  197.9 1.2 copy.186
  199.1 1.1 fusion.33
  200.2 6.8 %copy.188 = f32[3,24,8,128]{0,3,2,1:T(8,128)} copy(f32[3,24,8,128]{3,2,1,0:T(8,128)S(1)} %fusion.33) | data formatting | bytes 589824 | tf_op jit(solution)/shard_map/add | solution.py:179
  207.0 10.9 %scatter_fusion = f32[3,24576]{0,1:T(8,128)} fusion(f32[3,24576]{0,1:T(8,128)} %bitcast.222, s32[192]{0:T(256)S(1)} %bitcast.233, f32[192,3]{1,0:T(8,128)} %copy.200), kind=kCustom, calls=%fused_computation.7 | custom fusion | flops 576 | bytes 7680 | tf_op jit(solution)/shard_map/scatter-add | solution.py:126
  217.9 8.1 %copy.201 = f32[3,24,8,128]{3,2,1,0:T(8,128)} copy(f32[3,24,8,128]{0,3,2,1:T(8,128)} %bitcast.223) | data formatting | bytes 589824
  (199 shorter events, 52.4 us)
Async XLA Ops:
  1.4 107.2 %collective-permute-start.1 = (f32[3,1,8,128]{3,2,1,0:T(8,128)S(1)}, f32[3,1,8,128]{3,2,1,0:T(8,128)S(1)}, u32[]{:S(2)}, u32[]{:S(2)}) collective-permute-start(f32[3,1,8,128]{3,2,1,0:T(8,128)S(1)} %get-tuple-element.190), channel_id=1, source_target_pairs={{0,16},{16,32},{32,48},{48,64},{64,80},{80,96},{96,112},{112,128},... | collective-permute-start | bytes 36872 | tf_op jit(solution)/shard_map/ppermute | solution.py:21
  4.4 104.2 %collective-permute-start = (f32[3,1,8,128]{3,2,1,0:T(8,128)S(1)}, f32[3,1,8,128]{3,2,1,0:T(8,128)S(1)}, u32[]{:S(2)}, u32[]{:S(2)}) collective-permute-start(f32[3,1,8,128]{3,2,1,0:T(8,128)S(1)} %get-tuple-element.191), channel_id=1, source_target_pairs={{16,0},{32,16},{48,32},{64,48},{80,64},{96,80},{112,96},{128,112},... | collective-permute-start | bytes 36872 | tf_op jit(solution)/shard_map/ppermute | solution.py:24
  7.2 7.7 %copy-start.12 = (s32[32]{0:T(128)S(1)}, s32[32]{0:T(128)}, u32[]{:S(2)}) copy-start(s32[32]{0:T(128)} %param.12) | copy-start | bytes 388
  7.2 7.7 %copy-start.16 = (s32[32,1]{0,1:T(1,128)S(1)}, s32[32,1]{0,1:T(1,128)}, u32[]{:S(2)}) copy-start(s32[32,1]{0,1:T(1,128)} %param.13) | copy-start | bytes 388
  7.2 47.8 %copy-start.4 = (f32[24,8,128]{2,1,0:T(8,128)S(1)}, f32[24,8,128]{2,1,0:T(8,128)}, u32[]{:S(2)}) copy-start(f32[24,8,128]{2,1,0:T(8,128)} %param.11) | copy-start | bytes 294916
  7.3 53.4 %copy-start.1 = (f32[3,64,512]{2,1,0:T(8,128)S(1)}, f32[3,64,512]{2,1,0:T(8,128)}, u32[]{:S(2)}) copy-start(f32[3,64,512]{2,1,0:T(8,128)} %param.14) | copy-start | bytes 1179652
  47.7 12.9 %all-to-all-start = ((f32[9,32,2]{0,2,1:T(2,128)}), f32[9,32,2]{0,2,1:T(2,128)S(1)}, u32[]{:S(2)}, u32[]{:S(2)}) async-start(f32[9,32,2]{0,2,1:T(2,128)} %copy.197), calls=%async_computation | async-start | bytes 65536 | tf_op jit(solution)/shard_map/all_to_all | solution.py:167
  93.9 15.2 %copy-start = (f32[3,64,512]{2,1,0:T(8,128)}, f32[3,64,512]{2,1,0:T(8,128)S(1)}, u32[]{:S(2)}) copy-start(f32[3,64,512]{2,1,0:T(8,128)S(1)} %get-tuple-element.120) | copy-start | bytes 1179652
  93.9 14.6 %copy-start.3 = (f32[3,24,8,128]{3,2,1,0:T(8,128)S(1)}, f32[3,24,8,128]{3,2,1,0:T(8,128)}, u32[]{:S(2)}) copy-start(f32[3,24,8,128]{3,2,1,0:T(8,128)} %param.10) | copy-start | bytes 884740
  95.9 11.3 %all-to-all-start.1 = ((f32[6,32,2]{0,2,1:T(2,128)}), f32[6,32,2]{0,2,1:T(2,128)S(1)}, u32[]{:S(2)}, u32[]{:S(2)}) async-start(f32[6,32,2]{0,2,1:T(2,128)} %copy.199), calls=%async_computation.1 | async-start | bytes 65536 | tf_op jit(solution)/shard_map/all_to_all | solution.py:171
  109.9 10.9 %collective-permute-start.2 = (f32[3,26,1,128]{1,3,2,0:T(8,128)}, f32[3,26,1,128]{1,3,2,0:T(8,128)}, u32[]{:S(2)}, u32[]{:S(2)}) collective-permute-start(f32[3,26,1,128]{1,3,2,0:T(8,128)} %get-tuple-element.175), channel_id=1, source_target_pairs={{2,0},{4,2},{6,4},{8,6},{10,8},{12,10},{14,12},{3,1},{5,3},{7,5},{... | collective-permute-start | bytes 119816 | tf_op jit(solution)/shard_map/ppermute | solution.py:24
  112.0 9.7 %collective-permute-start.3 = (f32[3,26,1,128]{1,3,2,0:T(8,128)}, f32[3,26,1,128]{1,3,2,0:T(8,128)}, u32[]{:S(2)}, u32[]{:S(2)}) collective-permute-start(f32[3,26,1,128]{1,3,2,0:T(8,128)} %get-tuple-element.176), channel_id=1, source_target_pairs={{0,2},{2,4},{4,6},{6,8},{8,10},{10,12},{12,14},{1,3},{3,5},{5,7},{... | collective-permute-start | bytes 119816 | tf_op jit(solution)/shard_map/ppermute | solution.py:21
  120.9 5.9 %copy-start.2 = (f32[3,24,8,128]{1,3,2,0:T(8,128)S(1)}, f32[3,24,8,128]{1,3,2,0:T(8,128)}, u32[]{:S(2)}) copy-start(f32[3,24,8,128]{1,3,2,0:T(8,128)} %copy.202) | copy-start | bytes 884740
  122.4 4.6 %collective-permute-start.4 = (f32[3,26,10,1]{1,3,2,0:T(1,128)S(1)}, f32[3,26,10,1]{1,3,2,0:T(1,128)S(1)}, u32[]{:S(2)}, u32[]{:S(2)}) collective-permute-start(f32[3,26,10,1]{1,3,2,0:T(1,128)S(1)} %get-tuple-element.173), channel_id=1, source_target_pairs={{1,0},{3,2},{5,4},{7,6},{9,8},{11,10},{13,12},{15,14},{17,16},{19,... | collective-permute-start | bytes 9368 | tf_op jit(solution)/shard_map/ppermute | solution.py:24
  123.7 3.9 %collective-permute-start.5 = (f32[3,26,10,1]{1,3,2,0:T(1,128)S(1)}, f32[3,26,10,1]{1,3,2,0:T(1,128)S(1)}, u32[]{:S(2)}, u32[]{:S(2)}) collective-permute-start(f32[3,26,10,1]{1,3,2,0:T(1,128)S(1)} %get-tuple-element.174), channel_id=1, source_target_pairs={{0,1},{2,3},{4,5},{6,7},{8,9},{10,11},{12,13},{14,15},{16,17},{18,... | collective-permute-start | bytes 9368 | tf_op jit(solution)/shard_map/ppermute | solution.py:21
  127.0 3.3 %copy-start.7 = (f32[24,8,128]{0,2,1:T(8,128)S(1)}, f32[24,8,128]{0,2,1:T(8,128)}, u32[]{:S(2)}) copy-start(f32[24,8,128]{0,2,1:T(8,128)} %copy.157) | copy-start | bytes 294916
  131.4 6.7 %copy-start.19 = (f32[32]{0:T(128)S(1)}, f32[32]{0:T(128)}, u32[]{:S(2)}) copy-start(f32[32]{0:T(128)} %get-tuple-element.197) | copy-start | bytes 388
  131.4 7.3 %copy-start.18 = (f32[32]{0:T(128)S(1)}, f32[32]{0:T(128)}, u32[]{:S(2)}) copy-start(f32[32]{0:T(128)} %get-tuple-element.198) | copy-start | bytes 388
  131.4 8.0 %copy-start.17 = (f32[32]{0:T(128)S(1)}, f32[32]{0:T(128)}, u32[]{:S(2)}) copy-start(f32[32]{0:T(128)} %get-tuple-element.200) | copy-start | bytes 388
  132.1 11.9 %copy-start.5 = (f32[6,24,8,128]{3,2,1,0:T(8,128)}, f32[6,24,8,128]{3,2,1,0:T(8,128)S(1)}, u32[]{:S(2)}) copy-start(f32[6,24,8,128]{3,2,1,0:T(8,128)S(1)} %constant_dynamic-update-slice_fusion) | copy-start | bytes 1769476
  132.1 7.4 %collective-permute-start.7 = (f32[6,1,8,128]{3,2,1,0:T(8,128)S(1)}, f32[6,1,8,128]{3,2,1,0:T(8,128)S(1)}, u32[]{:S(2)}, u32[]{:S(2)}) collective-permute-start(f32[6,1,8,128]{3,2,1,0:T(8,128)S(1)} %get-tuple-element.186), channel_id=1, source_target_pairs={{0,16},{16,32},{32,48},{48,64},{64,80},{80,96},{96,112},{112,128},... | collective-permute-start | bytes 73736 | tf_op jit(solution)/shard_map/ppermute | solution.py:21
  136.1 7.8 %collective-permute-start.6 = (f32[6,1,8,128]{3,2,1,0:T(8,128)S(1)}, f32[6,1,8,128]{3,2,1,0:T(8,128)S(1)}, u32[]{:S(2)}, u32[]{:S(2)}) collective-permute-start(f32[6,1,8,128]{3,2,1,0:T(8,128)S(1)} %get-tuple-element.187), channel_id=1, source_target_pairs={{16,0},{32,16},{48,32},{64,48},{80,64},{96,80},{112,96},{128,112},... | collective-permute-start | bytes 73736 | tf_op jit(solution)/shard_map/ppermute | solution.py:24
  139.5 4.5 %copy-start.8 = (f32[6,1,8,128]{3,2,1,0:T(8,128)}, f32[6,1,8,128]{3,2,1,0:T(8,128)S(1)}, u32[]{:S(2)}) copy-start(f32[6,1,8,128]{3,2,1,0:T(8,128)S(1)} %collective-permute-done.7) | copy-start | bytes 73732
  144.0 0.6 copy-start.10
  147.4 8.5 %copy-start.14 = (f32[192]{0:T(256)S(1)}, f32[192]{0:T(256)}, u32[]{:S(2)}) copy-start(f32[192]{0:T(256)} %concatenate.129) | copy-start | bytes 2308
  147.5 8.5 %copy-start.15 = (f32[192]{0:T(256)S(1)}, f32[192]{0:T(256)}, u32[]{:S(2)}) copy-start(f32[192]{0:T(256)} %concatenate.131) | copy-start | bytes 2308
  148.4 13.3 %collective-permute-start.9 = (f32[6,26,1,128]{1,3,2,0:T(8,128)}, f32[6,26,1,128]{1,3,2,0:T(8,128)S(1)}, u32[]{:S(2)}, u32[]{:S(2)}) collective-permute-start(f32[6,26,1,128]{1,3,2,0:T(8,128)} %get-tuple-element.163), channel_id=1, source_target_pairs={{0,2},{2,4},{4,6},{6,8},{8,10},{10,12},{12,14},{1,3},{3,5},{5,7},{... | collective-permute-start | bytes 239624 | tf_op jit(solution)/shard_map/ppermute | solution.py:21
  154.0 13.1 %collective-permute-start.8 = (f32[6,26,1,128]{1,3,2,0:T(8,128)}, f32[6,26,1,128]{1,3,2,0:T(8,128)}, u32[]{:S(2)}, u32[]{:S(2)}) collective-permute-start(f32[6,26,1,128]{1,3,2,0:T(8,128)} %get-tuple-element.164), channel_id=1, source_target_pairs={{2,0},{4,2},{6,4},{8,6},{10,8},{12,10},{14,12},{3,1},{5,3},{7,5},{... | collective-permute-start | bytes 239624 | tf_op jit(solution)/shard_map/ppermute | solution.py:24
  156.7 17.3 %copy-start.6 = (f32[6,24,8,128]{3,2,1,0:T(8,128)S(1)}, f32[6,24,8,128]{3,2,1,0:T(8,128)}, u32[]{:S(2)}) copy-start(f32[6,24,8,128]{3,2,1,0:T(8,128)} %copy-done.5) | copy-start | bytes 1769476
  156.7 17.3 %copy-start.9 = (f32[6,1,8,128]{3,2,1,0:T(8,128)S(1)}, f32[6,1,8,128]{3,2,1,0:T(8,128)}, u32[]{:S(2)}) copy-start(f32[6,1,8,128]{3,2,1,0:T(8,128)} %copy-done.8) | copy-start | bytes 73732
  156.7 17.3 %copy-start.11 = (f32[6,1,8,128]{3,2,1,0:T(8,128)S(1)}, f32[6,1,8,128]{3,2,1,0:T(8,128)}, u32[]{:S(2)}) copy-start(f32[6,1,8,128]{3,2,1,0:T(8,128)} %copy-done.10) | copy-start | bytes 73732
  168.5 17.7 %collective-permute-start.10 = (f32[6,26,10,1]{1,3,2,0:T(1,128)}, f32[6,26,10,1]{1,3,2,0:T(1,128)}, u32[]{:S(2)}, u32[]{:S(2)}) collective-permute-start(f32[6,26,10,1]{1,3,2,0:T(1,128)} %get-tuple-element.161), channel_id=1, source_target_pairs={{1,0},{3,2},{5,4},{7,6},{9,8},{11,10},{13,12},{15,14},{17,16},{19,... | collective-permute-start | bytes 18728 | tf_op jit(solution)/shard_map/ppermute | solution.py:24
  169.8 16.4 %collective-permute-start.11 = (f32[6,26,10,1]{1,3,2,0:T(1,128)}, f32[6,26,10,1]{1,3,2,0:T(1,128)}, u32[]{:S(2)}, u32[]{:S(2)}) collective-permute-start(f32[6,26,10,1]{1,3,2,0:T(1,128)} %get-tuple-element.162), channel_id=1, source_target_pairs={{0,1},{2,3},{4,5},{6,7},{8,9},{10,11},{12,13},{14,15},{16,17},{18,... | collective-permute-start | bytes 18728 | tf_op jit(solution)/shard_map/ppermute | solution.py:21
  200.2 6.8 %copy-start.13 = (s32[192,1]{0,1:T(1,128)S(1)}, s32[192,1]{0,1:T(1,128)}, u32[]{:S(2)}) copy-start(s32[192,1]{0,1:T(1,128)} %compare_select_fusion) | copy-start | bytes 2308
where the time goes:
time: 229 us; the launch traced here: 226 us
  local copies, waits for them, and re-layouts  86.5 us (38%)
  other arithmetic  62.5 us (27%)
  starting transfers between devices  49.1 us (21%)
  waiting for transfers between devices  24.9 us (11%)
    add x32, other arithmetic, substep(): current[left_axis] + micro_step * drift_term  32 us
    unnamed x61, local copies, waits for them, and re-layouts  32 us
    ppermute x6, starting transfers between devices, padded_2(): lax.ppermute(lax.slice_in_dim(block, block.shape[dim] - width, None, axis...  24.9 us
    gather x6, local copies, waits for them, and re-layouts, shards(): upper_side = jnp.take(flat_velocity, flag_cell + stride, axis=1)  15.7 us
    gather x6, local copies, waits for them, and re-layouts, shards(): lower_side = jnp.take(flat_velocity, flag_cell - stride, axis=1)  15.7 us
    ppermute x6, starting transfers between devices, padded_2(): lax.ppermute(lax.slice_in_dim(block, 0, width, axis=dim), axis, backward)  11.2 us
    scatter-add x1, other arithmetic, add_polymer(): flattened = flattened.at[:, targets].add(updates)  10.9 us
    ppermute x6, waiting for transfers between devices, padded_2(): lax.ppermute(lax.slice_in_dim(block, 0, width, axis=dim), axis, backward)  9.81 us
  transfers between devices with their start and end apart: 14, of which 7 were waited for; matrix products, arithmetic and copies ran while one was open for 43% of the time, Pallas kernels for 0%

commit v1 on v0

v1 whole, which is shorter than its diff:
```python
import functools
import math

import jax
import jax.numpy as jnp
from jax import lax
from jax.experimental import pallas as pl
from jax.experimental.pallas import tpu as pltpu
from jax.sharding import PartitionSpec as P

MESH = pl.DeviceIdType.MESH
F32, BF16, I32 = jnp.float32, jnp.bfloat16, jnp.int32

PAIRS = ((0, 0), (1, 1), (2, 2), (0, 1), (0, 2), (1, 2))
SIDE = ((0, 3, 4), (3, 1, 5), (4, 5, 2))
SCALE = math.sqrt(200.0 / 30.0)

NX, NY, NZ = 24, 8, 128
ROWS = NX * NY
FLAG = 32
SLOTS = 64
BEADS = 512
STEPS = 16
BLOCK = 16
GROUP = BLOCK // 2
NBLOCK = SLOTS // BLOCK


def iota(shape, dim):
    return lax.broadcasted_iota(I32, shape, dim)


def pieces(x, count):
    out = []
    for _ in range(count):
        part = x.astype(BF16)
        out.append(part)
        x = x - part.astype(F32)
    return out


def dot(a, b):
    return jnp.dot(a, b, preferred_element_type=F32)


def kernel(
    n_macro, n_tile, n_micro,
    v_in, visc_in, cell_s_in, cell_in, owner_s_in, owner_in, conf_in, noise_in,
    vel_out, conf_out, fs_out,
    vp, visc, cells, cellv, owners, ownerv, rankv, ranks, q, nz, nf, gat, grow, vrow, prow,
    kst, kb, pol, send1, recv1, send2, recv2,
    yp1, zp1, hx1, hy1, hz1, sp, xp2, yp2, zp2, hx2, hy2, hz2, amat, vel,
    in_sem, out_sem, s1_sem, r1_sem, s2_sem, r2_sem, hs1_sem, hr1_sem, hs2_sem, hr2_sem,
):
    macro, tile, micro = lax.axis_index("macro"), lax.axis_index("tile"), lax.axis_index("micro")
    owners_n = n_macro * n_micro
    me = macro * n_micro + micro
    my_block = lax.div(me, GROUP)

    loads = [
        pltpu.make_async_copy(v_in, vp.at[:, pl.ds(NY, ROWS), :], in_sem.at[0]),
        pltpu.make_async_copy(cell_s_in, cells, in_sem.at[1]),
        pltpu.make_async_copy(cell_in, cellv, in_sem.at[2]),
        pltpu.make_async_copy(owner_s_in, owners, in_sem.at[3]),
        pltpu.make_async_copy(owner_in, ownerv, in_sem.at[4]),
        pltpu.make_async_copy(visc_in, visc, in_sem.at[5]),
        pltpu.make_async_copy(noise_in, nz, in_sem.at[6]),
        pltpu.make_async_copy(conf_in, q, in_sem.at[7]),
    ]
    for load in loads:
        load.start()

    barrier = pltpu.get_barrier_semaphore()

    def greet(k, carry):
        peer = lax.rem(me + k, owners_n)
        pl.semaphore_signal(
            barrier, inc=1,
            device_id=(lax.div(peer, n_micro), tile, lax.rem(peer, n_micro)), device_id_type=MESH,
        )
        return carry

    lax.fori_loop(1, owners_n, greet, 0)
    tile_up, tile_down = lax.rem(tile + 1, n_tile), lax.rem(tile + n_tile - 1, n_tile)
    macro_up, macro_down = lax.rem(macro + 1, n_macro), lax.rem(macro + n_macro - 1, n_macro)
    for target in (tile_up, tile_down):
        pl.semaphore_signal(barrier, inc=1, device_id=(macro, target, micro), device_id_type=MESH)

    for load in loads[:6]:
        load.wait()

    def gather(j, carry):
        row = lax.shift_right_logical(cells[j], 7) + NY
        for a in range(3):
            read = lambda offset: vp[a, pl.ds(row + offset, 1), :]
            gat[3 * a, pl.ds(j, 1), :] = read(NY) - read(-NY)
            gat[3 * a + 1, pl.ds(j, 1), :] = read(1) - read(-1)
            gat[3 * a + 2, pl.ds(j, 1), :] = read(0)
        gat[9, pl.ds(j, 1), :] = visc[pl.ds(row - NY, 1), :]
        return carry

    lax.fori_loop(0, FLAG, gather, 0, unroll=8)

    square0, square1 = iota((FLAG, FLAG), 0), iota((FLAG, FLAG), 1)

    def column(row):
        return jnp.sum(jnp.where(square0 == square1, row, 0), axis=1, keepdims=True)

    cell_row, owner_row = cellv[...], ownerv[...]
    cell_col, owner_col = column(cell_row), column(owner_row)
    z_col = cell_col & (NZ - 1)
    lane = iota((FLAG, NZ), 1)
    here, above, below = lane == z_col, lane == z_col + 1, lane == z_col - 1
    rank_row = jnp.sum(
        jnp.where((square0 < square1) & (owner_col == owner_row), 1, 0), axis=0, keepdims=True
    )
    rankv[...] = jnp.minimum(rank_row, 1)
    rank_copy = pltpu.make_async_copy(rankv, ranks, in_sem.at[8])
    rank_copy.start()

    gathered = jnp.zeros((FLAG, NZ), F32)
    columns = []
    for k in range(10):
        values = gat[k]
        if k < 9 and k % 3 == 2:
            picked = jnp.where(above, values, 0.0) - jnp.where(below, values, 0.0)
        else:
            picked = jnp.where(here, values, 0.0)
        if k < 9:
            picked = picked * 0.5
        columns.append(jnp.sum(picked, axis=1, keepdims=True))
        gathered = jnp.where(lane == k, columns[k], gathered)
    position = owner_row * 2 + rank_row
    placing = (iota((SLOTS, FLAG), 0) == position).astype(F32).astype(BF16)
    hi, mid, lo = pieces(gathered, 3)
    outgoing = dot(placing, hi) + (dot(placing, mid) + dot(placing, lo))
    for s in range(owners_n):
        send1[s] = outgoing[2 * s : 2 * s + 2, :]

    pl.semaphore_wait(barrier, owners_n + 1)

    def peer_id(peer):
        return (lax.div(peer, n_micro), tile, lax.rem(peer, n_micro))

    def block_of(order, sign):
        shift = (0, 1, NBLOCK - 1, 2)[order]
        return lax.rem(my_block + sign * shift + NBLOCK, NBLOCK)

    def post(block, send, recv, send_sem, recv_sem):
        def one(k, carry):
            peer = block * GROUP + lax.rem(me + k, GROUP)

            @pl.when(peer != me)
            def _():
                pltpu.make_async_remote_copy(
                    src_ref=send.at[peer], dst_ref=recv.at[me],
                    send_sem=send_sem, recv_sem=recv_sem.at[my_block],
                    device_id=peer_id(peer), device_id_type=MESH,
                ).start()

            @pl.when(peer == me)
            def _():
                pltpu.make_async_copy(send.at[me], recv.at[me], recv_sem.at[my_block]).start()

            return carry

        lax.fori_loop(0, GROUP, one, 0)

    def arrive(block, recv, recv_sem):
        part = recv.at[pl.ds(block * GROUP, GROUP)]
        pltpu.make_async_copy(part, part, recv_sem.at[block]).wait()

    def sent(send, send_sem):
        part = send.at[pl.ds(0, owners_n - 1)]
        pltpu.make_async_copy(part, part, send_sem).wait()

    for order in range(NBLOCK):
        post(block_of(order, -1), send1, recv1, s1_sem, r1_sem)

    sub, lanes = iota((NY, NZ), 0), iota((NY, NZ), 1)
    face = jnp.where(micro == 0, NZ - 1, 0)

    def pack_z(read):
        def one(x, carry):
            return tuple(
                total + pltpu.roll(jnp.where(lanes == face, value, 0.0), x, 1)
                for total, value in zip(carry, read(x))
            )

        return lax.fori_loop(0, NX, one, tuple(jnp.zeros((NY, NZ), F32) for _ in range(3)), unroll=4)

    for a in range(3):
        yp1[0, a] = vp[a, pl.ds(NY, NX, stride=NY), :]
        yp1[1, a] = vp[a, pl.ds(2 * NY - 1, NX, stride=NY), :]

    def rows_of(x):
        return pl.ds(pl.multiple_of((x + 1) * NY, NY), NY)

    packed = pack_z(lambda x: [vp[a, rows_of(x), :] for a in range(3)])
    for a in range(3):
        zp1[a] = packed[a]

    def halo_copies(x_low, x_high, y_pack, z_pack, hx, hy, hz, send_sem, recv_sem):
        def remote(i, src, dst, target):
            return pltpu.make_async_remote_copy(
                src_ref=src, dst_ref=dst, send_sem=send_sem.at[i], recv_sem=recv_sem.at[i],
                device_id=target, device_id_type=MESH,
            )

        return [
            remote(0, x_high, hx.at[0], (macro_up, tile, micro)),
            remote(1, x_low, hx.at[1], (macro_down, tile, micro)),
            remote(2, y_pack.at[1], hy.at[0], (macro, tile_up, micro)),
            remote(3, y_pack.at[0], hy.at[1], (macro, tile_down, micro)),
            remote(4, z_pack, hz, (macro, tile, 1 - micro)),
        ]

    halo1 = halo_copies(
        vp.at[:, pl.ds(NY, NY), :], vp.at[:, pl.ds(ROWS, NY), :], yp1, zp1, hx1, hy1, hz1, hs1_sem, hr1_sem
    )
    for copy in halo1:
        copy.start()

    loads[6].wait()

    def widen(t, carry):
        for a in range(3):
            nf[t, a] = nz[t, a].astype(F32) * (0.1 * SCALE)
        return carry

    lax.fori_loop(0, STEPS, widen, 0)
    loads[7].wait()
    for a in range(3):
        q[a] = q[a] * SCALE

    def chunk(c):
        return pl.ds(c * 128, 128)

    def block_work(order, carry):
        shift = jnp.where(order == 0, 0, jnp.where(order == 1, 1, jnp.where(order == 2, NBLOCK - 1, 2)))
        block = lax.rem(my_block + shift, NBLOCK)
        arrive(block, recv1, r1_sem)
        slots = pl.ds(pl.multiple_of(block * BLOCK, BLOCK), BLOCK)
        for s in range(GROUP):
            kst[pl.ds(2 * s, 2), :] = recv1[block * GROUP + s]
        kappa = kst[...] * 0.01
        for k in range(9):
            wide = jnp.broadcast_to(kappa[:, k : k + 1], (BLOCK, 128))
            kb[k] = wide + 1.0 if k % 4 == 0 else wide

        def step(t, state):
            new = []
            for c in range(BEADS // 128):
                q0, q1, q2 = state[3 * c : 3 * c + 3]
                pull = pltpu.reciprocal(
                    jnp.maximum(200.0 - q0 * q0 - (q1 * q1 + q2 * q2), 20.0), approx=True
                )
                for a in range(3):
                    here_q = (q0, q1, q2)[a]
                    other = [b for b in range(3) if b != a]
                    new.append(
                        (kb[4 * a] - pull) * here_q
                        + (kb[3 * a + other[0]] * (q0, q1, q2)[other[0]] + kb[3 * a + other[1]] * (q0, q1, q2)[other[1]])
                        + nf[t, a, slots, chunk(c)]
                    )
            return tuple(new)

        state = tuple(q[a, slots, chunk(c)] for c in range(BEADS // 128) for a in range(3))
        state = lax.fori_loop(0, STEPS, step, state, unroll=2)
        sums = [None] * 6
        for c in range(BEADS // 128):
            values = state[3 * c : 3 * c + 3]
            q0, q1, q2 = values
            pull = 1.0 / jnp.maximum(200.0 - (q0 * q0 + q1 * q1 + q2 * q2), 20.0)
            for a in range(3):
                q[a, slots, chunk(c)] = values[a] * (1.0 / SCALE)
            for k, (a, b) in enumerate(PAIRS):
                term = pull * values[a] * values[b]
                sums[k] = term if sums[k] is None else sums[k] + term
        lane16 = iota((BLOCK, 128), 1)
        stresses = jnp.zeros((BLOCK, 128), F32)
        for k, (a, b) in enumerate(PAIRS):
            mean = jnp.sum(sums[k], axis=1, keepdims=True) * (30.0 / BEADS)
            stresses = jnp.where(lane16 == k, 0.25 * (mean - (1.0 if a == b else 0.0)), stresses)
        pol[...] = stresses
        for s in range(GROUP):
            send2[block * GROUP + s] = pol[pl.ds(2 * s, 2), :]
        post(block, send2, recv2, s2_sem, r2_sem)
        pltpu.make_async_copy(q.at[:, slots, :], conf_out.at[:, slots, :], out_sem.at[0]).start()
        return carry

    lax.fori_loop(0, NBLOCK, block_work, 0)

    for copy in halo1:
        copy.wait()

    def keep(condition):
        return jnp.where(condition, 1.0, 0.0)

    x_low, x_high = keep(macro > 0), keep(macro < n_macro - 1)
    y_low, y_high = keep(tile > 0), keep(tile < n_tile - 1)
    first_lane, last_lane = lanes == 0, lanes == NZ - 1
    z_high, z_low = keep(micro == 0), keep(micro == 1)

    def slope_y(value, hy, a, x):
        low = hy[0, a, pl.ds(x, 1), :] * y_low
        high = hy[1, a, pl.ds(x, 1), :] * y_high
        up = jnp.where(sub == NY - 1, high, pltpu.roll(value, NY - 1, 0))
        down = jnp.where(sub == 0, low, pltpu.roll(value, 1, 0))
        return up - down

    def slope_z(value, hz, a, x):
        beside = pltpu.roll(hz[a], lax.rem(NZ - x, NZ), 1)
        up = pltpu.roll(jnp.where(first_lane, beside * z_high, value), NZ - 1, 1)
        down = pltpu.roll(jnp.where(last_lane, beside * z_low, value), 1, 1)
        return up - down

    for a in range(3):
        vp[a, pl.ds(0, NY), :] = hx1[0, a] * x_low
        vp[a, pl.ds(ROWS + NY, NY), :] = hx1[1, a] * x_high

    def stress_at(x, carry):
        grad = {}
        for a in range(3):
            value = vp[a, rows_of(x), :]
            grad[a, 0] = vp[a, rows_of(x + 1), :] - vp[a, rows_of(x - 1), :]
            grad[a, 1] = slope_y(value, hy1, a, x)
            grad[a, 2] = slope_z(value, hz1, a, x)
        half = visc[pl.ds(pl.multiple_of(x * NY, NY), NY), :] * 0.5
        for k, (a, b) in enumerate(PAIRS):
            sp[k, rows_of(x), :] = half * (grad[a, b] + grad[b, a])
        return carry

    lax.fori_loop(0, NX, stress_at, 0, unroll=2)

    for a in range(3):
        xp2[0, a] = sp[SIDE[0][a], pl.ds(NY, NY), :]
        xp2[1, a] = sp[SIDE[0][a], pl.ds(ROWS, NY), :]
        yp2[0, a] = sp[SIDE[1][a], pl.ds(NY, NX, stride=NY), :]
        yp2[1, a] = sp[SIDE[1][a], pl.ds(2 * NY - 1, NX, stride=NY), :]
    packed = pack_z(lambda x: [sp[SIDE[2][a], rows_of(x), :] for a in range(3)])
    for a in range(3):
        zp2[a] = packed[a]
    halo2 = halo_copies(xp2.at[0], xp2.at[1], yp2, zp2, hx2, hy2, hz2, hs2_sem, hr2_sem)
    for copy in halo2:
        copy.start()

    viscous = jnp.zeros((FLAG, NZ), F32)
    for k, (a, b) in enumerate(PAIRS):
        viscous = jnp.where(lane == k, columns[9] * (columns[3 * a + b] + columns[3 * b + a]), viscous)
    vrow[...] = viscous
    row_col = lax.shift_right_logical(cell_col, 7)
    six = jnp.concatenate([row_col] * 6, axis=0)
    wide0, wide1 = iota((ROWS, ROWS), 0), iota((ROWS, ROWS), 1)
    six_row = jnp.sum(jnp.where(wide0 == wide1, six, 0), axis=0, keepdims=True)
    offset = jnp.where(wide1 < 64, NY, jnp.where(wide1 < 128, 1, 0))
    plus = jnp.where(wide0 == six_row - offset, 1.0, 0.0)
    minus = jnp.where((wide0 == six_row + offset) & (wide1 < 128), 1.0, 0.0)
    amat[...] = (plus - minus).astype(BF16)

    for copy in halo2:
        copy.wait()
    for a in range(3):
        sp[SIDE[0][a], pl.ds(0, NY), :] = hx2[0, a] * x_low
        sp[SIDE[0][a], pl.ds(ROWS + NY, NY), :] = hx2[1, a] * x_high

    def advance_at(x, carry):
        for a in range(3):
            total = sp[SIDE[0][a], rows_of(x + 1), :] - sp[SIDE[0][a], rows_of(x - 1), :]
            total = total + slope_y(sp[SIDE[1][a], rows_of(x), :], hy2, a, x)
            total = total + slope_z(sp[SIDE[2][a], rows_of(x), :], hz2, a, x)
            vel[a, pl.ds(pl.multiple_of(x * NY, NY), NY), :] = vp[a, rows_of(x), :] + 0.05 * total
        return carry

    lax.fori_loop(0, NX, advance_at, 0, unroll=2)

    rank_copy.wait()
    for block in range(NBLOCK):
        arrive(block, recv2, r2_sem)

    def collect(j, carry):
        prow[pl.ds(j, 1), :] = recv2[owners[j], pl.ds(ranks[0, j], 1), :]
        return carry

    lax.fori_loop(0, FLAG, collect, 0, unroll=8)
    returned = prow[...]
    flagged = vrow[...] + jnp.where(lane < 6, returned, 0.0)
    pick = (iota((8, NZ), 0) == iota((8, NZ), 1)).astype(F32).astype(BF16)
    turned = None
    for part in pieces(flagged, 3):
        term = lax.dot_general(pick, part, (((1,), (1,)), ((), ())), preferred_element_type=F32)
        turned = term if turned is None else turned + term
    fs_out[...] = turned[:6, :]

    spread = [jnp.broadcast_to(returned[:, k : k + 1] * 0.05, (FLAG, NZ)) for k in range(6)]
    for a in range(3):
        parts = []
        parts += pieces(jnp.where(here, spread[SIDE[0][a]], 0.0), 2)
        parts += pieces(jnp.where(here, spread[SIDE[1][a]], 0.0), 2)
        parts += pieces(
            jnp.where(below, spread[SIDE[2][a]], 0.0) - jnp.where(above, spread[SIDE[2][a]], 0.0), 2
        )
        vel[a] = vel[a] + dot(amat[...], jnp.concatenate(parts, axis=0))
        pltpu.make_async_copy(vel.at[a], vel_out.at[a], out_sem.at[1]).start()

    pltpu.make_async_copy(vel, vel_out, out_sem.at[1]).wait()
    pltpu.make_async_copy(q, conf_out, out_sem.at[0]).wait()
    sent(send1, s1_sem)
    sent(send2, s2_sem)


def shards(sizes, velocity, viscosity, flag_cell, flag_owner, conformations, increments):
    owner = flag_owner.reshape(FLAG)
    any_spec = pl.BlockSpec(memory_space=pltpu.HBM)
    vmem = lambda *shape: pltpu.VMEM(shape, F32)
    scratch = [
        vmem(3, ROWS + 2 * NY, NZ), vmem(ROWS, NZ),
        pltpu.SMEM((FLAG,), I32), pltpu.VMEM((1, FLAG), I32),
        pltpu.SMEM((FLAG,), I32), pltpu.VMEM((1, FLAG), I32),
        pltpu.VMEM((1, FLAG), I32), pltpu.SMEM((1, FLAG), I32),
        vmem(3, SLOTS, BEADS),
        pltpu.VMEM((STEPS, 3, SLOTS, BEADS), BF16), vmem(STEPS, 3, SLOTS, BEADS),
        vmem(10, FLAG, NZ), vmem(FLAG, NZ), vmem(FLAG, NZ), vmem(FLAG, NZ),
        vmem(BLOCK, 128), vmem(9, BLOCK, 128), vmem(BLOCK, 128),
        vmem(32, 2, 128), vmem(32, 2, 128), vmem(32, 2, 128), vmem(32, 2, 128),
        vmem(2, 3, NX, NZ), vmem(3, NY, NZ), vmem(2, 3, NY, NZ), vmem(2, 3, NX, NZ), vmem(3, NY, NZ),
        vmem(6, ROWS + 2 * NY, NZ),
        vmem(2, 3, NY, NZ), vmem(2, 3, NX, NZ), vmem(3, NY, NZ),
        vmem(2, 3, NY, NZ), vmem(2, 3, NX, NZ), vmem(3, NY, NZ),
        pltpu.VMEM((ROWS, ROWS), BF16), vmem(3, ROWS, NZ),
        pltpu.SemaphoreType.DMA((9,)), pltpu.SemaphoreType.DMA((2,)),
        pltpu.SemaphoreType.DMA, pltpu.SemaphoreType.DMA((NBLOCK,)),
        pltpu.SemaphoreType.DMA, pltpu.SemaphoreType.DMA((NBLOCK,)),
        pltpu.SemaphoreType.DMA((5,)), pltpu.SemaphoreType.DMA((5,)),
        pltpu.SemaphoreType.DMA((5,)), pltpu.SemaphoreType.DMA((5,)),
    ]
    vel, conf, stress = pl.pallas_call(
        functools.partial(kernel, *sizes),
        out_shape=(
            jax.ShapeDtypeStruct((3, ROWS, NZ), F32),
            jax.ShapeDtypeStruct(conformations.shape, F32),
            jax.ShapeDtypeStruct((6, FLAG), F32),
        ),
        in_specs=[any_spec] * 8,
        out_specs=(any_spec, any_spec, pl.BlockSpec(memory_space=pltpu.VMEM)),
        scratch_shapes=scratch,
        compiler_params=pltpu.CompilerParams(
            collective_id=0, has_side_effects=True, vmem_limit_bytes=56 * 2**20
        ),
    )(
        velocity.reshape(3, ROWS, NZ), viscosity.reshape(ROWS, NZ),
        flag_cell, flag_cell.reshape(1, FLAG), owner, owner.reshape(1, FLAG),
        conformations, increments,
    )
    return vel.reshape(velocity.shape), conf, stress


def solution(mesh):
    sizes = (mesh.shape["macro"], mesh.shape["tile"], mesh.shape["micro"])
    in_specs = (
        P(None, "macro", "tile", "micro"),
        P("macro", "tile", "micro"),
        P(("macro", "tile", "micro")),
        P(("macro", "tile", "micro"), None),
        P(None, ("macro", "tile", "micro"), None),
        P(None, None, ("macro", "tile", "micro"), None),
    )
    out_specs = (
        P(None, "macro", "tile", "micro"),
        P(None, ("macro", "tile", "micro"), None),
        P(None, ("macro", "tile", "micro")),
    )
    return jax.shard_map(
        functools.partial(shards, sizes), mesh=mesh, in_specs=in_specs, out_specs=out_specs, check_vma=False
    )
```

time: 229 us -> 33.2 us (0.14)
  the two profiles are of different devices: /device:TPU:120 before, /device:TPU:1 now
where the time goes in v1:
time: 33.2 us; the launch traced here: 33 us
  Pallas kernels  27.6 us (83%)
  local copies, waits for them, and re-layouts  4.74 us (14%)
  between operations  0.64 us (2%)
    pallas_call x1, Pallas kernels, shards(): pl.pallas_call(functools.partial(kernel, *sizes), out_shape=(jax.ShapeDty...  27.6 us
    unnamed x3, local copies, waits for them, and re-layouts  4.74 us

profile of v1, /device:TPU:1, one launch (start us, length us, event | category | flops | bytes accessed | tf_op | source)
XLA Modules:
  0.0 33.0 jit_solution(6699298851919938471)
XLA Ops:
  0.6 27.6 %shard_map.85 = (f32[3,192,128]{2,1,0:T(8,128)}, f32[3,64,512]{2,1,0:T(8,128)}, f32[6,32]{1,0:T(8,128)}) custom-call(f32[3,192,128]{2,1,0:T(8,128)} %bitcast.6, f32[192,128]{1,0:T(8,128)} %bitcast.8, s32[32]{0:T(128)} %cell_s_in.1, s32[1,32]{1,0:T(1,128)} %bitcast.9, s32[32]{0:T(128)} %bitcast.10, s32[1,32]{1,0:T(1,128)} %bitcast.11, f32[3,64,512]{2,1,0:T(8,128)} %conf_in.1, ...), custom_call_target="tpu_custom_call" | custom-call | tf_op jit(solution)/shard_map/pallas_call | solution.py:437
  28.3 1.7 %copy.12 = f32[3,24,8,128]{3,2,1,0:T(8,128)} copy(f32[3,24,8,128]{3,2,1,0:T(8,128)} %bitcast.7) | data formatting | bytes 589824
  30.0 1.8 %copy.13 = f32[3,64,512]{2,1,0:T(8,128)} copy(f32[3,64,512]{2,1,0:T(8,128)} %get-tuple-element.13) | data formatting | bytes 786432
  31.7 1.3 %copy.14 = f32[6,32]{1,0:T(8,128)} copy(f32[6,32]{1,0:T(8,128)} %get-tuple-element.14) | data formatting | bytes 1536

commit v2 on v1

v2 whole, which is shorter than its diff:
```python
import functools
import math

import jax
import jax.numpy as jnp
from jax import lax
from jax.experimental import pallas as pl
from jax.experimental.pallas import tpu as pltpu
from jax.sharding import PartitionSpec as P

MESH = pl.DeviceIdType.MESH
F32, BF16, I32 = jnp.float32, jnp.bfloat16, jnp.int32

PAIRS = ((0, 0), (1, 1), (2, 2), (0, 1), (0, 2), (1, 2))
SIDE = ((0, 3, 4), (3, 1, 5), (4, 5, 2))
SCALE = math.sqrt(200.0 / 30.0)

NX, NY, NZ = 24, 8, 128
ROWS = NX * NY
FLAG = 32
SLOTS = 64
BEADS = 512
STEPS = 16
BLOCK = 16
GROUP = BLOCK // 2
NBLOCK = SLOTS // BLOCK
STRESS_AT = 2
UNROLL = 4


def iota(shape, dim):
    return lax.broadcasted_iota(I32, shape, dim)


def pieces(x, count):
    out = []
    for _ in range(count):
        part = x.astype(BF16)
        out.append(part)
        x = x - part.astype(F32)
    return out


def dot(a, b):
    return jnp.dot(a, b, preferred_element_type=F32)


def kernel(
    n_macro, n_tile, n_micro,
    v, visc, cells_in, cellv, owners_in, ownerv, conf, noise_in,
    vel_out, conf_out, fs_out,
    cells, owners, rankv, ranks, q, nz, nf, gat, vrow, prow,
    kst, kb, pol, send1, recv1, send2, recv2,
    yp1, zp1, hx1, hy1, hz1, sp, xp2, yp2, zp2, hx2, hy2, hz2, amat,
    in_sem, s1_sem, r1_sem, s2_sem, r2_sem, hs1_sem, hr1_sem, hs2_sem, hr2_sem,
):
    macro, tile, micro = lax.axis_index("macro"), lax.axis_index("tile"), lax.axis_index("micro")
    owners_n = n_macro * n_micro
    me = macro * n_micro + micro
    my_block = lax.div(me, GROUP)

    loads = [
        pltpu.make_async_copy(cells_in, cells, in_sem.at[0]),
        pltpu.make_async_copy(owners_in, owners, in_sem.at[1]),
        pltpu.make_async_copy(noise_in, nz, in_sem.at[2]),
    ]
    for load in loads:
        load.start()

    barrier = pltpu.get_barrier_semaphore()
    has_up, has_down = tile < n_tile - 1, tile > 0

    def peer_id(peer):
        return (lax.div(peer, n_micro), tile, lax.rem(peer, n_micro))

    def greet(k, carry):
        pl.semaphore_signal(
            barrier, inc=1, device_id=peer_id(lax.rem(me + k, owners_n)), device_id_type=MESH
        )
        return carry

    lax.fori_loop(1, owners_n, greet, 0, unroll=True)

    @pl.when(has_up)
    def _():
        pl.semaphore_signal(barrier, inc=1, device_id=(macro, tile + 1, micro), device_id_type=MESH)

    @pl.when(has_down)
    def _():
        pl.semaphore_signal(barrier, inc=1, device_id=(macro, tile - 1, micro), device_id_type=MESH)

    loads[0].wait()

    def gather(j, carry):
        row = lax.shift_right_logical(cells[j], 7)
        row = jnp.minimum(jnp.maximum(row, NY), ROWS - NY - 1)
        for a in range(3):
            read = lambda offset: v[a, pl.ds(row + offset, 1), :]
            gat[3 * a, pl.ds(j, 1), :] = read(NY) - read(-NY)
            gat[3 * a + 1, pl.ds(j, 1), :] = read(1) - read(-1)
            gat[3 * a + 2, pl.ds(j, 1), :] = read(0)
        gat[9, pl.ds(j, 1), :] = visc[pl.ds(row, 1), :]
        return carry

    lax.fori_loop(0, FLAG, gather, 0, unroll=8)

    square0, square1 = iota((FLAG, FLAG), 0), iota((FLAG, FLAG), 1)

    def column(row):
        return jnp.sum(jnp.where(square0 == square1, row, 0), axis=1, keepdims=True)

    cell_row, owner_row = cellv[...], ownerv[...]
    cell_col, owner_col = column(cell_row), column(owner_row)
    z_col = cell_col & (NZ - 1)
    lane = iota((FLAG, NZ), 1)
    here, above, below = lane == z_col, lane == z_col + 1, lane == z_col - 1
    rank_row = jnp.sum(
        jnp.where((square0 < square1) & (owner_col == owner_row), 1, 0), axis=0, keepdims=True
    )
    rankv[...] = jnp.minimum(rank_row, 1)
    rank_copy = pltpu.make_async_copy(rankv, ranks, in_sem.at[3])
    rank_copy.start()

    gathered = jnp.zeros((FLAG, NZ), F32)
    columns = []
    for k in range(10):
        values = gat[k]
        if k < 9 and k % 3 == 2:
            picked = jnp.where(above, values, 0.0) - jnp.where(below, values, 0.0)
        else:
            picked = jnp.where(here, values, 0.0)
        if k < 9:
            picked = picked * 0.5
        columns.append(jnp.sum(picked, axis=1, keepdims=True))
        if k < 9:
            gathered = jnp.where(lane == k, columns[k], gathered)
    position = owner_row * 2 + rank_row
    placing = (iota((SLOTS, FLAG), 0) == position).astype(F32).astype(BF16)
    hi, mid, lo = pieces(gathered, 3)
    outgoing = dot(placing, hi) + (dot(placing, mid) + dot(placing, lo))
    for s in range(owners_n):
        send1[s] = outgoing[2 * s : 2 * s + 2, :]

    @pl.when(has_up & has_down)
    def _():
        pl.semaphore_wait(barrier, owners_n + 1)

    @pl.when(jnp.logical_not(has_up & has_down))
    def _():
        pl.semaphore_wait(barrier, owners_n)

    def block_of(order, sign):
        shift = (0, 1, NBLOCK - 1, 2)[order]
        return lax.rem(my_block + sign * shift + NBLOCK, NBLOCK)

    def post(order, block, send, recv, send_sem, recv_sem):
        if order == 0:
            recv[me] = send[me]
        base = block * GROUP
        turn = me - my_block * GROUP
        for k in range(1 if order == 0 else 0, GROUP):
            peer = base + lax.rem(turn + k, GROUP)
            pltpu.make_async_remote_copy(
                src_ref=send.at[peer], dst_ref=recv.at[me],
                send_sem=send_sem, recv_sem=recv_sem.at[my_block],
                device_id=peer_id(peer), device_id_type=MESH,
            ).start()

    def arrive(order, block, recv, recv_sem):
        part = recv.at[pl.ds(0, GROUP - 1 if order == 0 else GROUP)]
        pltpu.make_async_copy(part, part, recv_sem.at[block]).wait()

    def sent(send, send_sem):
        part = send.at[pl.ds(0, owners_n - 1)]
        pltpu.make_async_copy(part, part, send_sem).wait()

    for order in range(NBLOCK):
        post(order, block_of(order, -1), send1, recv1, s1_sem, r1_sem)

    sub, lanes = iota((NY, NZ), 0), iota((NY, NZ), 1)
    face = lanes == jnp.where(micro == 0, NZ - 1, 0)
    first_lane, last_lane = lanes == 0, lanes == NZ - 1
    first_row, last_row = sub == 0, sub == NY - 1

    def rows_of(x):
        return pl.ds(x * NY, NY)

    def pack(source, names, y_pack, z_pack):
        for a, name in enumerate(names[1]):
            y_pack[0, a] = source[name, pl.ds(0, NX, stride=NY), :]
            y_pack[1, a] = source[name, pl.ds(NY - 1, NX, stride=NY), :]
        for a, name in enumerate(names[2]):
            totals = [None, None, None, None]
            for x in range(NX):
                term = jnp.where(face, source[name, rows_of(x), :], 0.0)
                if x:
                    term = pltpu.roll(term, 2 * x, 1)
                totals[x % 4] = term if totals[x % 4] is None else totals[x % 4] + term
            z_pack[a] = (totals[0] + totals[1]) + (totals[2] + totals[3])

    def exchange(x_low, x_high, y_pack, z_pack, hx, hy, hz, send_sem, recv_sem):
        def remote(i, src, dst, target):
            return pltpu.make_async_remote_copy(
                src_ref=src, dst_ref=dst, send_sem=send_sem.at[i], recv_sem=recv_sem.at[i],
                device_id=target, device_id_type=MESH,
            )

        moves = [
            (macro < n_macro - 1, macro > 0, remote(0, x_high, hx.at[0], (macro + 1, tile, micro)), hx.at[0]),
            (macro > 0, macro < n_macro - 1, remote(1, x_low, hx.at[1], (macro - 1, tile, micro)), hx.at[1]),
            (has_up, has_down, remote(2, y_pack.at[1], hy.at[0], (macro, tile + 1, micro)), hy.at[0]),
            (has_down, has_up, remote(3, y_pack.at[0], hy.at[1], (macro, tile - 1, micro)), hy.at[1]),
        ]
        beside = remote(4, z_pack, hz, (macro, tile, 1 - micro))

        def start():
            for sends, _, copy, _ in moves:
                pl.when(sends)(copy.start)
            beside.start()

        def finish():
            for _, comes, copy, landing in moves:
                pl.when(comes)(copy.wait_recv)

                @pl.when(jnp.logical_not(comes))
                def _():
                    landing[...] = jnp.zeros(landing.shape, F32)

            beside.wait_recv()

        def drain():
            for sends, _, copy, _ in moves:
                pl.when(sends)(copy.wait_send)
            beside.wait_send()

        return start, finish, drain

    def slope_x(source, name, hx, a, x):
        up = source[name, rows_of(x + 1), :] if x < NX - 1 else hx[1, a]
        down = source[name, rows_of(x - 1), :] if x > 0 else hx[0, a]
        return up - down

    def slope_y(source, name, hy, a, x):
        if x < NX - 1:
            up = source[name, pl.ds(x * NY + 1, NY), :]
        else:
            up = pltpu.roll(source[name, rows_of(x), :], NY - 1, 0)
        if x > 0:
            down = source[name, pl.ds(x * NY - 1, NY), :]
        else:
            down = pltpu.roll(source[name, rows_of(x), :], 1, 0)
        up = jnp.where(last_row, hy[1, a, pl.ds(x, 1), :], up)
        return up - jnp.where(first_row, hy[0, a, pl.ds(x, 1), :], down)

    def slope_z(source, name, hz, a, x):
        value, beside = source[name, rows_of(x), :], hz[a]
        if x:
            beside = pltpu.roll(beside, NZ - 2 * x, 1)
        up = pltpu.roll(jnp.where(first_lane, beside, value), NZ - 1, 1)
        return up - pltpu.roll(jnp.where(last_lane, beside, value), 1, 1)

    pack(v, ((0, 1, 2),) * 3, yp1, zp1)
    start1, finish1, drain1 = exchange(
        v.at[:, pl.ds(0, NY), :], v.at[:, pl.ds(ROWS - NY, NY), :], yp1, zp1, hx1, hy1, hz1, hs1_sem, hr1_sem
    )
    start2, finish2, drain2 = exchange(
        xp2.at[0], xp2.at[1], yp2, zp2, hx2, hy2, hz2, hs2_sem, hr2_sem
    )
    start1()

    loads[2].wait()

    def widen(t, carry):
        for a in range(3):
            nf[t, a] = nz[t, a].astype(F32) * (0.1 * SCALE)
        return carry

    lax.fori_loop(0, STEPS, widen, 0)
    for a in range(3):
        q[a] = conf[a] * SCALE

    def chunk(c):
        return pl.ds(c * 128, 128)

    def block_work(order):
        block = block_of(order, 1)
        arrive(order, block, recv1, r1_sem)
        slots = pl.ds(pl.multiple_of(block * BLOCK, BLOCK), BLOCK)
        for s in range(GROUP):
            kst[pl.ds(2 * s, 2), :] = recv1[block * GROUP + s]
        kappa = kst[...] * 0.01
        for k in range(9):
            wide = jnp.broadcast_to(kappa[:, k : k + 1], (BLOCK, 128))
            kb[k] = wide + 1.0 if k % 4 == 0 else wide

        def step(t, state):
            new = []
            for c in range(BEADS // 128):
                q0, q1, q2 = state[3 * c : 3 * c + 3]
                pull = pltpu.reciprocal(
                    jnp.maximum(200.0 - q0 * q0 - (q1 * q1 + q2 * q2), 20.0), approx=True
                )
                for a in range(3):
                    here_q = (q0, q1, q2)[a]
                    other = [b for b in range(3) if b != a]
                    new.append(
                        (kb[4 * a] - pull) * here_q
                        + (kb[3 * a + other[0]] * (q0, q1, q2)[other[0]] + kb[3 * a + other[1]] * (q0, q1, q2)[other[1]])
                        + nf[t, a, slots, chunk(c)]
                    )
            return tuple(new)

        state = tuple(q[a, slots, chunk(c)] for c in range(BEADS // 128) for a in range(3))
        state = lax.fori_loop(0, STEPS, step, state, unroll=UNROLL)
        sums = [None] * 6
        for c in range(BEADS // 128):
            values = state[3 * c : 3 * c + 3]
            q0, q1, q2 = values
            pull = 1.0 / jnp.maximum(200.0 - (q0 * q0 + q1 * q1 + q2 * q2), 20.0)
            for a in range(3):
                conf_out[a, slots, chunk(c)] = values[a] * (1.0 / SCALE)
            pulled = [pull * value for value in values]
            for k, (a, b) in enumerate(PAIRS):
                term = pulled[a] * values[b]
                sums[k] = term if sums[k] is None else sums[k] + term
        lane16 = iota((BLOCK, 128), 1)
        stresses = jnp.zeros((BLOCK, 128), F32)
        for k, (a, b) in enumerate(PAIRS):
            mean = jnp.sum(sums[k], axis=1, keepdims=True) * (30.0 / BEADS)
            stresses = jnp.where(lane16 == k, 0.25 * (mean - (1.0 if a == b else 0.0)), stresses)
        pol[...] = stresses
        for s in range(GROUP):
            send2[block * GROUP + s] = pol[pl.ds(2 * s, 2), :]
        post(order, block, send2, recv2, s2_sem, r2_sem)

    def stress_work():
        finish1()
        for x in range(NX):
            grad = {}
            for a in range(3):
                grad[a, 0] = slope_x(v, a, hx1, a, x)
                grad[a, 1] = slope_y(v, a, hy1, a, x)
                grad[a, 2] = slope_z(v, a, hz1, a, x)
            half = visc[rows_of(x), :] * 0.5
            for k, (a, b) in enumerate(PAIRS):
                sp[k, rows_of(x), :] = half * (grad[a, b] + grad[b, a])
        for a in range(3):
            xp2[0, a] = sp[SIDE[0][a], rows_of(0), :]
            xp2[1, a] = sp[SIDE[0][a], rows_of(NX - 1), :]
        pack(sp, SIDE, yp2, zp2)
        start2()

    for order in range(NBLOCK):
        if order == STRESS_AT:
            stress_work()
        block_work(order)
    if STRESS_AT == NBLOCK:
        stress_work()

    viscous = jnp.zeros((FLAG, NZ), F32)
    for k, (a, b) in enumerate(PAIRS):
        viscous = jnp.where(lane == k, columns[9] * (columns[3 * a + b] + columns[3 * b + a]), viscous)
    vrow[...] = viscous
    row_col = lax.shift_right_logical(cell_col, 7)
    six = jnp.concatenate([row_col] * 6, axis=0)
    wide0, wide1 = iota((ROWS, ROWS), 0), iota((ROWS, ROWS), 1)
    six_row = jnp.sum(jnp.where(wide0 == wide1, six, 0), axis=0, keepdims=True)
    offset = jnp.where(wide1 < 64, NY, jnp.where(wide1 < 128, 1, 0))
    plus = jnp.where(wide0 == six_row - offset, 1.0, 0.0)
    minus = jnp.where((wide0 == six_row + offset) & (wide1 < 128), 1.0, 0.0)
    amat[...] = (plus - minus).astype(BF16)

    finish2()
    for x in range(NX):
        for a in range(3):
            total = slope_x(sp, SIDE[0][a], hx2, a, x)
            total = total + slope_y(sp, SIDE[1][a], hy2, a, x)
            total = total + slope_z(sp, SIDE[2][a], hz2, a, x)
            vel_out[a, rows_of(x), :] = v[a, rows_of(x), :] + 0.05 * total

    loads[1].wait()
    rank_copy.wait()
    for order in range(NBLOCK):
        arrive(order, block_of(order, 1), recv2, r2_sem)

    def collect(j, carry):
        prow[pl.ds(j, 1), :] = recv2[owners[j], pl.ds(ranks[0, j], 1), :]
        return carry

    lax.fori_loop(0, FLAG, collect, 0, unroll=8)
    returned = prow[...]
    flagged = vrow[...] + jnp.where(lane < 6, returned, 0.0)
    pick = (iota((8, NZ), 0) == iota((8, NZ), 1)).astype(F32).astype(BF16)
    turned = None
    for part in pieces(flagged, 3):
        term = lax.dot_general(pick, part, (((1,), (1,)), ((), ())), preferred_element_type=F32)
        turned = term if turned is None else turned + term
    fs_out[...] = turned[:6, :]

    spread = [jnp.broadcast_to(returned[:, k : k + 1] * 0.05, (FLAG, NZ)) for k in range(6)]
    for a in range(3):
        parts = []
        parts += pieces(jnp.where(here, spread[SIDE[0][a]], 0.0), 2)
        parts += pieces(jnp.where(here, spread[SIDE[1][a]], 0.0), 2)
        parts += pieces(
            jnp.where(below, spread[SIDE[2][a]], 0.0) - jnp.where(above, spread[SIDE[2][a]], 0.0), 2
        )
        vel_out[a] = vel_out[a] + dot(amat[...], jnp.concatenate(parts, axis=0))

    drain1()
    drain2()
    sent(send1, s1_sem)
    sent(send2, s2_sem)


def write_out(vel, conf, stress, vel_out, conf_out, stress_out, sem):
    copies = [
        pltpu.make_async_copy(source, target, sem.at[i])
        for i, (source, target) in enumerate(((conf, conf_out), (vel, vel_out), (stress, stress_out)))
    ]
    for copy in copies:
        copy.start()
    for copy in copies:
        copy.wait()


def shards(sizes, velocity, viscosity, flag_cell, flag_owner, conformations, increments):
    owner = flag_owner.reshape(FLAG)
    hbm = pl.BlockSpec(memory_space=pl.ANY)
    here = pl.BlockSpec(memory_space=pltpu.VMEM)
    vmem = lambda *shape: pltpu.VMEM(shape, F32)
    scratch = [
        pltpu.SMEM((FLAG,), I32), pltpu.SMEM((FLAG,), I32),
        pltpu.VMEM((1, FLAG), I32), pltpu.SMEM((1, FLAG), I32),
        vmem(3, SLOTS, BEADS),
        pltpu.VMEM((STEPS, 3, SLOTS, BEADS), BF16), vmem(STEPS, 3, SLOTS, BEADS),
        vmem(10, FLAG, NZ), vmem(FLAG, NZ), vmem(FLAG, NZ),
        vmem(BLOCK, 128), vmem(9, BLOCK, 128), vmem(BLOCK, 128),
        vmem(32, 2, 128), vmem(32, 2, 128), vmem(32, 2, 128), vmem(32, 2, 128),
        vmem(2, 3, NX, NZ), vmem(3, NY, NZ), vmem(2, 3, NY, NZ), vmem(2, 3, NX, NZ), vmem(3, NY, NZ),
        vmem(6, ROWS, NZ),
        vmem(2, 3, NY, NZ), vmem(2, 3, NX, NZ), vmem(3, NY, NZ),
        vmem(2, 3, NY, NZ), vmem(2, 3, NX, NZ), vmem(3, NY, NZ),
        pltpu.VMEM((ROWS, ROWS), BF16),
        pltpu.SemaphoreType.DMA((4,)),
        pltpu.SemaphoreType.DMA, pltpu.SemaphoreType.DMA((NBLOCK,)),
        pltpu.SemaphoreType.DMA, pltpu.SemaphoreType.DMA((NBLOCK,)),
        pltpu.SemaphoreType.DMA((5,)), pltpu.SemaphoreType.DMA((5,)),
        pltpu.SemaphoreType.DMA((5,)), pltpu.SemaphoreType.DMA((5,)),
    ]
    shapes = (
        jax.ShapeDtypeStruct((3, ROWS, NZ), F32),
        jax.ShapeDtypeStruct(conformations.shape, F32),
        jax.ShapeDtypeStruct((6, FLAG), F32),
    )
    results = pl.pallas_call(
        functools.partial(kernel, *sizes),
        out_shape=shapes,
        in_specs=[here, here, hbm, here, hbm, here, here, hbm],
        out_specs=(here, here, here),
        scratch_shapes=scratch,
        compiler_params=pltpu.CompilerParams(
            collective_id=0, has_side_effects=True, vmem_limit_bytes=52 * 2**20
        ),
    )(
        velocity.reshape(3, ROWS, NZ), viscosity.reshape(ROWS, NZ),
        flag_cell, flag_cell.reshape(1, FLAG), owner, owner.reshape(1, FLAG),
        conformations, increments,
    )
    vel, conf, stress = pl.pallas_call(
        write_out,
        out_shape=shapes,
        in_specs=[here] * 3,
        out_specs=(hbm,) * 3,
        scratch_shapes=[pltpu.SemaphoreType.DMA((3,))],
        compiler_params=pltpu.CompilerParams(vmem_limit_bytes=4 * 2**20),
    )(*results)
    return vel.reshape(velocity.shape), conf, stress


def solution(mesh):
    sizes = (mesh.shape["macro"], mesh.shape["tile"], mesh.shape["micro"])
    in_specs = (
        P(None, "macro", "tile", "micro"),
        P("macro", "tile", "micro"),
        P(("macro", "tile", "micro")),
        P(("macro", "tile", "micro"), None),
        P(None, ("macro", "tile", "micro"), None),
        P(None, None, ("macro", "tile", "micro"), None),
    )
    out_specs = (
        P(None, "macro", "tile", "micro"),
        P(None, ("macro", "tile", "micro"), None),
        P(None, ("macro", "tile", "micro")),
    )
    return jax.shard_map(
        functools.partial(shards, sizes), mesh=mesh, in_specs=in_specs, out_specs=out_specs, check_vma=False
    )
```

time: 33.2 us -> 26.1 us (0.79)
  Pallas kernels: 27.6 us -> 21.1 us
  local copies, waits for them, and re-layouts: 4.74 us -> 4.15 us
    pallas_call x1 -> x2, Pallas kernels: 27.6 us -> 21.1 us  [the longest x1 20.2 us: shards(): pl.pallas_call(functools.partial(kernel, *sizes), out_shape=shapes, in_sp...]
    unnamed x3 -> x10, local copies, waits for them, and re-layouts: 4.74 us -> 4.15 us
where the time goes in v2:
time: 26.1 us; the launch traced here: 25.9 us
  Pallas kernels  21.1 us (81%)
  local copies, waits for them, and re-layouts  4.15 us (16%)
  between operations  0.65 us (2%)
    pallas_call x1, Pallas kernels, shards(): pl.pallas_call(functools.partial(kernel, *sizes), out_shape=shapes, in_sp...  20.2 us
    unnamed x10, local copies, waits for them, and re-layouts  4.15 us
    pallas_call x1, Pallas kernels, shards(): pl.pallas_call(write_out, out_shape=shapes, in_specs=[here] * 3, out_spec...  0.87 us

profile of v2, /device:TPU:1, one launch (start us, length us, event | category | flops | bytes accessed | tf_op | source)
XLA Modules:
  0.0 25.9 jit_solution(10442066345616533017)
XLA Ops:
  0.6 0.0 copy-start
  0.6 1.0 %copy-done = f32[3,64,512]{2,1,0:T(8,128)S(1)} copy-done((f32[3,64,512]{2,1,0:T(8,128)S(1)}, f32[3,64,512]{2,1,0:T(8,128)}, u32[]{:S(2)}) %copy-start) | copy-done | bytes 393240
  1.6 0.0 copy-start.1
  1.6 1.0 %copy-done.1 = f32[3,24,8,128]{3,2,1,0:T(8,128)S(1)} copy-done((f32[3,24,8,128]{3,2,1,0:T(8,128)S(1)}, f32[3,24,8,128]{3,2,1,0:T(8,128)}, u32[]{:S(2)}) %copy-start.1) | copy-done | bytes 294936
  2.6 0.0 copy-start.2
  2.6 0.9 %copy-done.2 = f32[24,8,128]{2,1,0:T(8,128)S(1)} copy-done((f32[24,8,128]{2,1,0:T(8,128)S(1)}, f32[24,8,128]{2,1,0:T(8,128)}, u32[]{:S(2)}) %copy-start.2) | copy-done | bytes 98328
  3.5 0.0 copy-start.3
  3.5 0.7 %copy-done.3 = s32[32]{0:T(128)S(1)} copy-done((s32[32]{0:T(128)S(1)}, s32[32]{0:T(128)}, u32[]{:S(2)}) %copy-start.3) | copy-done | bytes 152
  4.1 0.0 copy-start.4
  4.1 0.7 %copy-done.4 = s32[32,1]{0,1:T(1,128)S(1)} copy-done((s32[32,1]{0,1:T(1,128)S(1)}, s32[32,1]{0,1:T(1,128)}, u32[]{:S(2)}) %copy-start.4) | copy-done | bytes 152
  4.8 20.2 %shard_map.85 = (f32[3,192,128]{2,1,0:T(8,128)S(1)}, f32[3,64,512]{2,1,0:T(8,128)S(1)}, f32[6,32]{1,0:T(8,128)S(1)}) custom-call(f32[3,192,128]{2,1,0:T(8,128)S(1)} %bitcast.6, f32[192,128]{1,0:T(8,128)S(1)} %bitcast.7, s32[32]{0:T(128)S(1)} %copy-done.3, s32[1,32]{1,0:T(1,128)S(1)} %bitcast.8, s32[32]{0:T(128)S(1)} %bitcast.9, s32[1,32]{1,0:T(1,128)S(1)} %bitcast.10, ...), custom_call_target="tpu_custom_call" | custom-call | tf_op jit(solution)/shard_map/pallas_call | solution.py:456
  25.0 0.9 %shard_map.86 = (f32[3,192,128]{2,1,0:T(8,128)}, f32[3,64,512]{2,1,0:T(8,128)}, f32[6,32]{1,0:T(8,128)}) custom-call(f32[3,192,128]{2,1,0:T(8,128)S(1)} %get-tuple-element.9.vel, f32[3,64,512]{2,1,0:T(8,128)S(1)} %get-tuple-element.10.conf, f32[6,32]{1,0:T(8,128)S(1)} %get-tuple-element.11.stress), custom_call_target="tpu_custom_call" | custom-call | tf_op jit(solution)/shard_map/pallas_call | solution.py:470
Async XLA Ops:
  0.6 1.0 %copy-start = (f32[3,64,512]{2,1,0:T(8,128)S(1)}, f32[3,64,512]{2,1,0:T(8,128)}, u32[]{:S(2)}) copy-start(f32[3,64,512]{2,1,0:T(8,128)} %conf.1) | copy-start | bytes 1179652
  1.6 1.0 %copy-start.1 = (f32[3,24,8,128]{3,2,1,0:T(8,128)S(1)}, f32[3,24,8,128]{3,2,1,0:T(8,128)}, u32[]{:S(2)}) copy-start(f32[3,24,8,128]{3,2,1,0:T(8,128)} %param.6) | copy-start | bytes 884740
  2.6 0.9 %copy-start.2 = (f32[24,8,128]{2,1,0:T(8,128)S(1)}, f32[24,8,128]{2,1,0:T(8,128)}, u32[]{:S(2)}) copy-start(f32[24,8,128]{2,1,0:T(8,128)} %param.7) | copy-start | bytes 294916
  3.5 0.7 %copy-start.3 = (s32[32]{0:T(128)S(1)}, s32[32]{0:T(128)}, u32[]{:S(2)}) copy-start(s32[32]{0:T(128)} %cells_in.1) | copy-start | bytes 388
  4.1 0.7 %copy-start.4 = (s32[32,1]{0,1:T(1,128)S(1)}, s32[32,1]{0,1:T(1,128)}, u32[]{:S(2)}) copy-start(s32[32,1]{0,1:T(1,128)} %param.9) | copy-start | bytes 388

commit v3 on v2

--- a/solution.py
+++ b/solution.py
@@ -41,18 +41,23 @@
     return out
 
 
+def column(row):
+    diagonal = iota((FLAG, FLAG), 0) == iota((FLAG, FLAG), 1)
+    return jnp.sum(jnp.where(diagonal, row, 0), axis=1, keepdims=True)
+
+
 def dot(a, b):
     return jnp.dot(a, b, preferred_element_type=F32)
 
 
 def kernel(
     n_macro, n_tile, n_micro,
-    v, visc, cells_in, cellv, owners_in, ownerv, conf, noise_in,
-    vel_out, conf_out, fs_out,
-    cells, owners, rankv, ranks, q, nz, nf, gat, vrow, prow,
-    kst, kb, pol, send1, recv1, send2, recv2,
+    v_in, visc_in, cells_in, cell_in, owner_in, conf_in, noise_in,
+    vel_out, conf_out, recv2, amat_out, vrow_out, rank_out,
+    v, visc, cells, cellv, ownerv, rankv, q, nz, nf, gat, vrow, vel,
+    kst, kb, pol, send1, recv1, send2,
     yp1, zp1, hx1, hy1, hz1, sp, xp2, yp2, zp2, hx2, hy2, hz2, amat,
-    in_sem, s1_sem, r1_sem, s2_sem, r2_sem, hs1_sem, hr1_sem, hs2_sem, hr2_sem,
+    in_sem, out_sem, s1_sem, r1_sem, s2_sem, r2_sem, hs1_sem, hr1_sem, hs2_sem, hr2_sem,
 ):
     macro, tile, micro = lax.axis_index("macro"), lax.axis_index("tile"), lax.axis_index("micro")
     owners_n = n_macro * n_micro
@@ -60,9 +65,13 @@
     my_block = lax.div(me, GROUP)
 
     loads = [
-        pltpu.make_async_copy(cells_in, cells, in_sem.at[0]),
-        pltpu.make_async_copy(owners_in, owners, in_sem.at[1]),
-        pltpu.make_async_copy(noise_in, nz, in_sem.at[2]),
+        pltpu.make_async_copy(v_in, v, in_sem.at[0]),
+        pltpu.make_async_copy(cells_in, cells, in_sem.at[1]),
+        pltpu.make_async_copy(cell_in, cellv, in_sem.at[2]),
+        pltpu.make_async_copy(owner_in, ownerv, in_sem.at[3]),
+        pltpu.make_async_copy(visc_in, visc, in_sem.at[4]),
+        pltpu.make_async_copy(noise_in, nz, in_sem.at[5]),
+        pltpu.make_async_copy(conf_in, q, in_sem.at[6]),
     ]
     for load in loads:
         load.start()
@@ -89,7 +98,8 @@
     def _():
         pl.semaphore_signal(barrier, inc=1, device_id=(macro, tile - 1, micro), device_id_type=MESH)
 
-    loads[0].wait()
+    for load in loads[:5]:
+        load.wait()
 
     def gather(j, carry):
         row = lax.shift_right_logical(cells[j], 7)
@@ -105,10 +115,6 @@
     lax.fori_loop(0, FLAG, gather, 0, unroll=8)
 
     square0, square1 = iota((FLAG, FLAG), 0), iota((FLAG, FLAG), 1)
-
-    def column(row):
-        return jnp.sum(jnp.where(square0 == square1, row, 0), axis=1, keepdims=True)
-
     cell_row, owner_row = cellv[...], ownerv[...]
     cell_col, owner_col = column(cell_row), column(owner_row)
     z_col = cell_col & (NZ - 1)
@@ -118,7 +124,7 @@
         jnp.where((square0 < square1) & (owner_col == owner_row), 1, 0), axis=0, keepdims=True
     )
     rankv[...] = jnp.minimum(rank_row, 1)
-    rank_copy = pltpu.make_async_copy(rankv, ranks, in_sem.at[3])
+    rank_copy = pltpu.make_async_copy(rankv, rank_out, out_sem.at[0])
     rank_copy.start()
 
     gathered = jnp.zeros((FLAG, NZ), F32)
@@ -153,9 +159,9 @@
         shift = (0, 1, NBLOCK - 1, 2)[order]
         return lax.rem(my_block + sign * shift + NBLOCK, NBLOCK)
 
-    def post(order, block, send, recv, send_sem, recv_sem):
+    def post(order, block, send, recv, send_sem, recv_sem, own):
         if order == 0:
-            recv[me] = send[me]
+            own(me)
         base = block * GROUP
         turn = me - my_block * GROUP
         for k in range(1 if order == 0 else 0, GROUP):
@@ -174,8 +180,14 @@
         part = send.at[pl.ds(0, owners_n - 1)]
         pltpu.make_async_copy(part, part, send_sem).wait()
 
+    def keep_row(i):
+        recv1[i] = send1[i]
+
+    def own_row(i):
+        return pltpu.make_async_copy(send2.at[i], recv2.at[i], out_sem.at[1])
+
     for order in range(NBLOCK):
-        post(order, block_of(order, -1), send1, recv1, s1_sem, r1_sem)
+        post(order, block_of(order, -1), send1, recv1, s1_sem, r1_sem, keep_row)
 
     sub, lanes = iota((NY, NZ), 0), iota((NY, NZ), 1)
     face = lanes == jnp.where(micro == 0, NZ - 1, 0)
@@ -268,7 +280,7 @@
     )
     start1()
 
-    loads[2].wait()
+    loads[5].wait()
 
     def widen(t, carry):
         for a in range(3):
@@ -276,8 +288,9 @@
         return carry
 
     lax.fori_loop(0, STEPS, widen, 0)
+    loads[6].wait()
     for a in range(3):
-        q[a] = conf[a] * SCALE
+        q[a] = q[a] * SCALE
 
     def chunk(c):
         return pl.ds(c * 128, 128)
@@ -318,7 +331,7 @@
             q0, q1, q2 = values
             pull = 1.0 / jnp.maximum(200.0 - (q0 * q0 + q1 * q1 + q2 * q2), 20.0)
             for a in range(3):
-                conf_out[a, slots, chunk(c)] = values[a] * (1.0 / SCALE)
+                q[a, slots, chunk(c)] = values[a] * (1.0 / SCALE)
             pulled = [pull * value for value in values]
             for k, (a, b) in enumerate(PAIRS):
                 term = pulled[a] * values[b]
@@ -331,7 +344,7 @@
         pol[...] = stresses
         for s in range(GROUP):
             send2[block * GROUP + s] = pol[pl.ds(2 * s, 2), :]
-        post(order, block, send2, recv2, s2_sem, r2_sem)
+        post(order, block, send2, recv2, s2_sem, r2_sem, lambda i: own_row(i).start())
 
     def stress_work():
         finish1()
@@ -361,6 +374,8 @@
     for k, (a, b) in enumerate(PAIRS):
         viscous = jnp.where(lane == k, columns[9] * (columns[3 * a + b] + columns[3 * b + a]), viscous)
     vrow[...] = viscous
+    vrow_copy = pltpu.make_async_copy(vrow, vrow_out, out_sem.at[2])
+    vrow_copy.start()
     row_col = lax.shift_right_logical(cell_col, 7)
     six = jnp.concatenate([row_col] * 6, axis=0)
     wide0, wide1 = iota((ROWS, ROWS), 0), iota((ROWS, ROWS), 1)
@@ -369,6 +384,10 @@
     plus = jnp.where(wide0 == six_row - offset, 1.0, 0.0)
     minus = jnp.where((wide0 == six_row + offset) & (wide1 < 128), 1.0, 0.0)
     amat[...] = (plus - minus).astype(BF16)
+    amat_copy = pltpu.make_async_copy(amat, amat_out, out_sem.at[3])
+    amat_copy.start()
+    conf_copy = pltpu.make_async_copy(q, conf_out, out_sem.at[4])
+    conf_copy.start()
 
     finish2()
     for x in range(NX):
@@ -376,18 +395,48 @@
             total = slope_x(sp, SIDE[0][a], hx2, a, x)
             total = total + slope_y(sp, SIDE[1][a], hy2, a, x)
             total = total + slope_z(sp, SIDE[2][a], hz2, a, x)
-            vel_out[a, rows_of(x), :] = v[a, rows_of(x), :] + 0.05 * total
-
-    loads[1].wait()
-    rank_copy.wait()
+            vel[a, rows_of(x), :] = v[a, rows_of(x), :] + 0.05 * total
+
+    vel_copy = pltpu.make_async_copy(vel, vel_out, out_sem.at[5])
+    vel_copy.start()
+
+    drain1()
+    drain2()
+    sent(send1, s1_sem)
+    sent(send2, s2_sem)
+    for copy in (rank_copy, vrow_copy, amat_copy, conf_copy, vel_copy, own_row(me)):
+        copy.wait()
     for order in range(NBLOCK):
         arrive(order, block_of(order, 1), recv2, r2_sem)
 
+
+def finish(
+    vel_in, conf_in, back_in, amat_in, vrow_in, rank_in, cell_in, owners_in,
+    vel_out, conf_out, fs_out,
+    conf, vel, back, amat, vrow, ranks, cellv, owners, prow, stress, in_sem, out_sem,
+):
+    loads = [
+        pltpu.make_async_copy(source, target, in_sem.at[i])
+        for i, (source, target) in enumerate(
+            (
+                (back_in, back), (rank_in, ranks), (owners_in, owners), (cell_in, cellv),
+                (vrow_in, vrow), (amat_in, amat), (vel_in, vel), (conf_in, conf),
+            )
+        )
+    ]
+    for load in loads:
+        load.start()
+    for load in loads[:5]:
+        load.wait()
+
     def collect(j, carry):
-        prow[pl.ds(j, 1), :] = recv2[owners[j], pl.ds(ranks[0, j], 1), :]
+        prow[pl.ds(j, 1), :] = back[owners[j], pl.ds(ranks[0, j], 1), :]
         return carry
 
-    lax.fori_loop(0, FLAG, collect, 0, unroll=8)
+    lax.fori_loop(0, FLAG, collect, 0, unroll=True)
+    lane = iota((FLAG, NZ), 1)
+    z_col = column(cellv[...]) & (NZ - 1)
+    here, above, below = lane == z_col, lane == z_col + 1, lane == z_col - 1
     returned = prow[...]
     flagged = vrow[...] + jnp.where(lane < 6, returned, 0.0)
     pick = (iota((8, NZ), 0) == iota((8, NZ), 1)).astype(F32).astype(BF16)
@@ -395,9 +444,16 @@
     for part in pieces(flagged, 3):
         term = lax.dot_general(pick, part, (((1,), (1,)), ((), ())), preferred_element_type=F32)
         turned = term if turned is None else turned + term
-    fs_out[...] = turned[:6, :]
+    stress[...] = turned[:6, :]
+    stress_copy = pltpu.make_async_copy(stress, fs_out, out_sem.at[1])
+    stress_copy.start()
 
     spread = [jnp.broadcast_to(returned[:, k : k + 1] * 0.05, (FLAG, NZ)) for k in range(6)]
+    loads[7].wait()
+    conf_copy = pltpu.make_async_copy(conf, conf_out, out_sem.at[0])
+    conf_copy.start()
+    for load in loads[5:7]:
+        load.wait()
     for a in range(3):
         parts = []
         parts += pieces(jnp.where(here, spread[SIDE[0][a]], 0.0), 2)
@@ -405,76 +461,68 @@
         parts += pieces(
             jnp.where(below, spread[SIDE[2][a]], 0.0) - jnp.where(above, spread[SIDE[2][a]], 0.0), 2
         )
-        vel_out[a] = vel_out[a] + dot(amat[...], jnp.concatenate(parts, axis=0))
-
-    drain1()
-    drain2()
-    sent(send1, s1_sem)
-    sent(send2, s2_sem)
-
-
-def write_out(vel, conf, stress, vel_out, conf_out, stress_out, sem):
-    copies = [
-        pltpu.make_async_copy(source, target, sem.at[i])
-        for i, (source, target) in enumerate(((conf, conf_out), (vel, vel_out), (stress, stress_out)))
-    ]
-    for copy in copies:
-        copy.start()
-    for copy in copies:
-        copy.wait()
+        vel[a] = vel[a] + dot(amat[...], jnp.concatenate(parts, axis=0))
+        pltpu.make_async_copy(vel.at[a], vel_out.at[a], out_sem.at[2]).start()
+    conf_copy.wait()
+    stress_copy.wait()
+    pltpu.make_async_copy(vel, vel_out, out_sem.at[2]).wait()
 
 
 def shards(sizes, velocity, viscosity, flag_cell, flag_owner, conformations, increments):
     owner = flag_owner.reshape(FLAG)
+    cell_row, owner_row = flag_cell.reshape(1, FLAG), flag_owner.reshape(1, FLAG)
     hbm = pl.BlockSpec(memory_space=pl.ANY)
-    here = pl.BlockSpec(memory_space=pltpu.VMEM)
     vmem = lambda *shape: pltpu.VMEM(shape, F32)
+    shape = jax.ShapeDtypeStruct
     scratch = [
-        pltpu.SMEM((FLAG,), I32), pltpu.SMEM((FLAG,), I32),
-        pltpu.VMEM((1, FLAG), I32), pltpu.SMEM((1, FLAG), I32),
+        vmem(3, ROWS, NZ), vmem(ROWS, NZ),
+        pltpu.SMEM((FLAG,), I32), pltpu.VMEM((1, FLAG), I32), pltpu.VMEM((1, FLAG), I32), pltpu.VMEM((1, FLAG), I32),
         vmem(3, SLOTS, BEADS),
         pltpu.VMEM((STEPS, 3, SLOTS, BEADS), BF16), vmem(STEPS, 3, SLOTS, BEADS),
-        vmem(10, FLAG, NZ), vmem(FLAG, NZ), vmem(FLAG, NZ),
+        vmem(10, FLAG, NZ), vmem(FLAG, NZ), vmem(3, ROWS, NZ),
         vmem(BLOCK, 128), vmem(9, BLOCK, 128), vmem(BLOCK, 128),
-        vmem(32, 2, 128), vmem(32, 2, 128), vmem(32, 2, 128), vmem(32, 2, 128),
+        vmem(32, 2, 128), vmem(32, 2, 128), vmem(32, 2, 128),
         vmem(2, 3, NX, NZ), vmem(3, NY, NZ), vmem(2, 3, NY, NZ), vmem(2, 3, NX, NZ), vmem(3, NY, NZ),
         vmem(6, ROWS, NZ),
         vmem(2, 3, NY, NZ), vmem(2, 3, NX, NZ), vmem(3, NY, NZ),
         vmem(2, 3, NY, NZ), vmem(2, 3, NX, NZ), vmem(3, NY, NZ),
         pltpu.VMEM((ROWS, ROWS), BF16),
-        pltpu.SemaphoreType.DMA((4,)),
+        pltpu.SemaphoreType.DMA((7,)), pltpu.SemaphoreType.DMA((6,)),
         pltpu.SemaphoreType.DMA, pltpu.SemaphoreType.DMA((NBLOCK,)),
         pltpu.SemaphoreType.DMA, pltpu.SemaphoreType.DMA((NBLOCK,)),
         pltpu.SemaphoreType.DMA((5,)), pltpu.SemaphoreType.DMA((5,)),
         pltpu.SemaphoreType.DMA((5,)), pltpu.SemaphoreType.DMA((5,)),
     ]
-    shapes = (
-        jax.ShapeDtypeStruct((3, ROWS, NZ), F32),
-        jax.ShapeDtypeStruct(conformations.shape, F32),
-        jax.ShapeDtypeStruct((6, FLAG), F32),
-    )
-    results = pl.pallas_call(
+    vel, conf = shape((3, ROWS, NZ), F32), shape(conformations.shape, F32)
+    held = pl.pallas_call(
         functools.partial(kernel, *sizes),
-        out_shape=shapes,
-        in_specs=[here, here, hbm, here, hbm, here, here, hbm],
-        out_specs=(here, here, here),
+        out_shape=(
+            vel, conf, shape((32, 2, 128), F32), shape((ROWS, ROWS), BF16), shape((FLAG, NZ), F32),
+            shape((1, FLAG), I32),
+        ),
+        in_specs=[hbm] * 7,
+        out_specs=(hbm,) * 6,
         scratch_shapes=scratch,
         compiler_params=pltpu.CompilerParams(
-            collective_id=0, has_side_effects=True, vmem_limit_bytes=52 * 2**20
+            collective_id=0, has_side_effects=True, vmem_limit_bytes=56 * 2**20
         ),
     )(
         velocity.reshape(3, ROWS, NZ), viscosity.reshape(ROWS, NZ),
-        flag_cell, flag_cell.reshape(1, FLAG), owner, owner.reshape(1, FLAG),
-        conformations, increments,
+        flag_cell, cell_row, owner_row, conformations, increments,
     )
     vel, conf, stress = pl.pallas_call(
-        write_out,
-        out_shape=shapes,
-        in_specs=[here] * 3,
+        finish,
+        out_shape=(vel, conf, shape((6, FLAG), F32)),
+        in_specs=[hbm] * 8,
         out_specs=(hbm,) * 3,
-        scratch_shapes=[pltpu.SemaphoreType.DMA((3,))],
-        compiler_params=pltpu.CompilerParams(vmem_limit_bytes=4 * 2**20),
-    )(*results)
+        scratch_shapes=[
+            vmem(3, SLOTS, BEADS), vmem(3, ROWS, NZ), vmem(32, 2, 128), pltpu.VMEM((ROWS, ROWS), BF16), vmem(FLAG, NZ),
+            pltpu.SMEM((1, FLAG), I32), pltpu.VMEM((1, FLAG), I32), pltpu.SMEM((FLAG,), I32),
+            vmem(FLAG, NZ), vmem(6, FLAG),
+            pltpu.SemaphoreType.DMA((8,)), pltpu.SemaphoreType.DMA((3,)),
+        ],
+        compiler_params=pltpu.CompilerParams(vmem_limit_bytes=56 * 2**20),
+    )(*held, cell_row, owner)
     return vel.reshape(velocity.shape), conf, stress
 
 

time: 26.1 us -> 23.7 us (0.908)
  the two profiles are of different devices: /device:TPU:1 before, /device:TPU:96 now
where the time goes in v3:
time: 23.7 us; the launch traced here: 23.6 us
  Pallas kernels  23 us (97%)
  between operations  0.64 us (3%)
    pallas_call x1, Pallas kernels, shards(): pl.pallas_call(functools.partial(kernel, *sizes), out_shape=(vel, conf, s...  20.8 us
    pallas_call x1, Pallas kernels, shards(): pl.pallas_call(finish, out_shape=(vel, conf, shape((6, FLAG), F32)), in_s...  2.2 us

profile of v3, /device:TPU:96, one launch (start us, length us, event | category | flops | bytes accessed | tf_op | source)
XLA Modules:
  0.0 23.6 jit_solution(12494979532956648010)
XLA Ops:
  0.6 20.8 %shard_map.85 = (f32[3,192,128]{2,1,0:T(8,128)}, f32[3,64,512]{2,1,0:T(8,128)}, f32[32,2,128]{2,1,0:T(2,128)}, bf16[192,192]{1,0:T(8,128)(2,1)}, f32[32,128]{1,0:T(8,128)}, /*index=5*/s32[1,32]{1,0:T(1,128)}) custom-call(f32[3,192,128]{2,1,0:T(8,128)} %bitcast.6, f32[192,128]{1,0:T(8,128)} %bitcast.7, s32[32]{0:T(128)} %cells_in.1, s32[1,32]{1,0:T(1,128)} %bitcast.8, ...), custom_call_target="tpu_custom_call" | custom-call | tf_op jit(solution)/shard_map/pallas_call | solution.py:497
  21.4 2.2 %shard_map.86 = (f32[3,192,128]{2,1,0:T(8,128)}, f32[3,64,512]{2,1,0:T(8,128)}, f32[6,32]{1,0:T(8,128)}) custom-call(f32[3,192,128]{2,1,0:T(8,128)} %get-tuple-element.12.vel_in, f32[3,64,512]{2,1,0:T(8,128)} %get-tuple-element.13.conf_in, f32[32,2,128]{2,1,0:T(2,128)} %get-tuple-element.14.back_in, bf16[192,192]{1,0:T(8,128)(2,1)} %get-tuple-element.15.amat_in, ...), custom_call_target="tpu_custom_call" | custom-call | tf_op jit(solution)/shard_map/pallas_call | solution.py:513

commit v4 on v3

--- a/solution.py
+++ b/solution.py
@@ -24,8 +24,8 @@
 BLOCK = 16
 GROUP = BLOCK // 2
 NBLOCK = SLOTS // BLOCK
-STRESS_AT = 2
-UNROLL = 4
+STRESS_AT = 1
+UNROLL = 8
 
 
 def iota(shape, dim):
@@ -56,7 +56,7 @@
     vel_out, conf_out, recv2, amat_out, vrow_out, rank_out,
     v, visc, cells, cellv, ownerv, rankv, q, nz, nf, gat, vrow, vel,
     kst, kb, pol, send1, recv1, send2,
-    yp1, zp1, hx1, hy1, hz1, sp, xp2, yp2, zp2, hx2, hy2, hz2, amat,
+    yp1, zp1, hx1, hy1, hz1, sp, xp2, yp2, zp2, hx2, hy2, hz2, amat, layers,
     in_sem, out_sem, s1_sem, r1_sem, s2_sem, r2_sem, hs1_sem, hr1_sem, hs2_sem, hr2_sem,
 ):
     macro, tile, micro = lax.axis_index("macro"), lax.axis_index("tile"), lax.axis_index("micro")
@@ -265,11 +265,14 @@
         return up - jnp.where(first_row, hy[0, a, pl.ds(x, 1), :], down)
 
     def slope_z(source, name, hz, a, x):
-        value, beside = source[name, rows_of(x), :], hz[a]
-        if x:
-            beside = pltpu.roll(beside, NZ - 2 * x, 1)
+        value, beside = source[name, rows_of(x), :], hz[a, rows_of(x), :]
         up = pltpu.roll(jnp.where(first_lane, beside, value), NZ - 1, 1)
         return up - pltpu.roll(jnp.where(last_lane, beside, value), 1, 1)
+
+    def unpack(hz, layers):
+        for a in range(3):
+            for x in range(NX):
+                layers[a, rows_of(x), :] = pltpu.roll(hz[a], NZ - 2 * x, 1) if x else hz[a]
 
     pack(v, ((0, 1, 2),) * 3, yp1, zp1)
     start1, finish1, drain1 = exchange(
@@ -348,12 +351,13 @@
 
     def stress_work():
         finish1()
+        unpack(hz1, layers)
         for x in range(NX):
             grad = {}
             for a in range(3):
                 grad[a, 0] = slope_x(v, a, hx1, a, x)
                 grad[a, 1] = slope_y(v, a, hy1, a, x)
-                grad[a, 2] = slope_z(v, a, hz1, a, x)
+                grad[a, 2] = slope_z(v, a, layers, a, x)
             half = visc[rows_of(x), :] * 0.5
             for k, (a, b) in enumerate(PAIRS):
                 sp[k, rows_of(x), :] = half * (grad[a, b] + grad[b, a])
@@ -390,11 +394,12 @@
     conf_copy.start()
 
     finish2()
+    unpack(hz2, layers)
     for x in range(NX):
         for a in range(3):
             total = slope_x(sp, SIDE[0][a], hx2, a, x)
             total = total + slope_y(sp, SIDE[1][a], hy2, a, x)
-            total = total + slope_z(sp, SIDE[2][a], hz2, a, x)
+            total = total + slope_z(sp, SIDE[2][a], layers, a, x)
             vel[a, rows_of(x), :] = v[a, rows_of(x), :] + 0.05 * total
 
     vel_copy = pltpu.make_async_copy(vel, vel_out, out_sem.at[5])
@@ -486,7 +491,7 @@
         vmem(6, ROWS, NZ),
         vmem(2, 3, NY, NZ), vmem(2, 3, NX, NZ), vmem(3, NY, NZ),
         vmem(2, 3, NY, NZ), vmem(2, 3, NX, NZ), vmem(3, NY, NZ),
-        pltpu.VMEM((ROWS, ROWS), BF16),
+        pltpu.VMEM((ROWS, ROWS), BF16), vmem(3, ROWS, NZ),
         pltpu.SemaphoreType.DMA((7,)), pltpu.SemaphoreType.DMA((6,)),
         pltpu.SemaphoreType.DMA, pltpu.SemaphoreType.DMA((NBLOCK,)),
         pltpu.SemaphoreType.DMA, pltpu.SemaphoreType.DMA((NBLOCK,)),

time: 23.7 us -> 21.6 us (0.911)
  the two profiles are of different devices: /device:TPU:96 before, /device:TPU:1 now
where the time goes in v4:
time: 21.6 us; the launch traced here: 21.4 us
  Pallas kernels  20.7 us (96%)
  between operations  0.64 us (3%)
    pallas_call x1, Pallas kernels, shards(): pl.pallas_call(functools.partial(kernel, *sizes), out_shape=(vel, conf, s...  18.5 us
    pallas_call x1, Pallas kernels, shards(): pl.pallas_call(finish, out_shape=(vel, conf, shape((6, FLAG), F32)), in_s...  2.2 us

profile of v4, /device:TPU:1, one launch (start us, length us, event | category | flops | bytes accessed | tf_op | source)
XLA Modules:
  0.0 21.4 jit_solution(2694465084485562354)
XLA Ops:
  0.6 18.5 %shard_map.85 = (f32[3,192,128]{2,1,0:T(8,128)}, f32[3,64,512]{2,1,0:T(8,128)}, f32[32,2,128]{2,1,0:T(2,128)}, bf16[192,192]{1,0:T(8,128)(2,1)}, f32[32,128]{1,0:T(8,128)}, /*index=5*/s32[1,32]{1,0:T(1,128)}) custom-call(f32[3,192,128]{2,1,0:T(8,128)} %bitcast.6, f32[192,128]{1,0:T(8,128)} %bitcast.7, s32[32]{0:T(128)} %cells_in.1, s32[1,32]{1,0:T(1,128)} %bitcast.8, ...), custom_call_target="tpu_custom_call" | custom-call | tf_op jit(solution)/shard_map/pallas_call | solution.py:502
  19.2 2.2 %shard_map.86 = (f32[3,192,128]{2,1,0:T(8,128)}, f32[3,64,512]{2,1,0:T(8,128)}, f32[6,32]{1,0:T(8,128)}) custom-call(f32[3,192,128]{2,1,0:T(8,128)} %get-tuple-element.12.vel_in, f32[3,64,512]{2,1,0:T(8,128)} %get-tuple-element.13.conf_in, f32[32,2,128]{2,1,0:T(2,128)} %get-tuple-element.14.back_in, bf16[192,192]{1,0:T(8,128)(2,1)} %get-tuple-element.15.amat_in, ...), custom_call_target="tpu_custom_call" | custom-call | tf_op jit(solution)/shard_map/pallas_call | solution.py:518

commit v5 on v4

--- a/solution.py
+++ b/solution.py
@@ -26,6 +26,7 @@
 NBLOCK = SLOTS // BLOCK
 STRESS_AT = 1
 UNROLL = 8
+SHIFTS = (0, 2, 1, 3)
 
 
 def iota(shape, dim):
@@ -156,15 +157,15 @@
         pl.semaphore_wait(barrier, owners_n)
 
     def block_of(order, sign):
-        shift = (0, 1, NBLOCK - 1, 2)[order]
+        shift = SHIFTS[order]
         return lax.rem(my_block + sign * shift + NBLOCK, NBLOCK)
 
     def post(order, block, send, recv, send_sem, recv_sem, own):
-        if order == 0:
+        if SHIFTS[order] == 0:
             own(me)
         base = block * GROUP
         turn = me - my_block * GROUP
-        for k in range(1 if order == 0 else 0, GROUP):
+        for k in range(1 if SHIFTS[order] == 0 else 0, GROUP):
             peer = base + lax.rem(turn + k, GROUP)
             pltpu.make_async_remote_copy(
                 src_ref=send.at[peer], dst_ref=recv.at[me],
@@ -173,7 +174,7 @@
             ).start()
 
     def arrive(order, block, recv, recv_sem):
-        part = recv.at[pl.ds(0, GROUP - 1 if order == 0 else GROUP)]
+        part = recv.at[pl.ds(0, GROUP - 1 if SHIFTS[order] == 0 else GROUP)]
         pltpu.make_async_copy(part, part, recv_sem.at[block]).wait()
 
     def sent(send, send_sem):

time: 21.6 us -> 20.9 us (0.968)
  Pallas kernels: 20.7 us -> 20.1 us
    pallas_call x1, Pallas kernels: 18.5 us -> 17.9 us  [shards(): pl.pallas_call(functools.partial(kernel, *sizes), out_shape=(vel, conf, s...]
where the time goes in v5:
time: 20.9 us; the launch traced here: 20.8 us
  Pallas kernels  20.1 us (96%)
  between operations  0.64 us (3%)
    pallas_call x1, Pallas kernels, shards(): pl.pallas_call(functools.partial(kernel, *sizes), out_shape=(vel, conf, s...  17.9 us
    pallas_call x1, Pallas kernels, shards(): pl.pallas_call(finish, out_shape=(vel, conf, shape((6, FLAG), F32)), in_s...  2.2 us

profile of v5, /device:TPU:1, one launch (start us, length us, event | category | flops | bytes accessed | tf_op | source)
XLA Modules:
  0.0 20.8 jit_solution(10373329588383704224)
XLA Ops:
  0.6 17.9 %shard_map.85 = (f32[3,192,128]{2,1,0:T(8,128)}, f32[3,64,512]{2,1,0:T(8,128)}, f32[32,2,128]{2,1,0:T(2,128)}, bf16[192,192]{1,0:T(8,128)(2,1)}, f32[32,128]{1,0:T(8,128)}, /*index=5*/s32[1,32]{1,0:T(1,128)}) custom-call(f32[3,192,128]{2,1,0:T(8,128)} %bitcast.6, f32[192,128]{1,0:T(8,128)} %bitcast.7, s32[32]{0:T(128)} %cells_in.1, s32[1,32]{1,0:T(1,128)} %bitcast.8, ...), custom_call_target="tpu_custom_call" | custom-call | tf_op jit(solution)/shard_map/pallas_call | solution.py:503
  18.6 2.2 %shard_map.86 = (f32[3,192,128]{2,1,0:T(8,128)}, f32[3,64,512]{2,1,0:T(8,128)}, f32[6,32]{1,0:T(8,128)}) custom-call(f32[3,192,128]{2,1,0:T(8,128)} %get-tuple-element.12.vel_in, f32[3,64,512]{2,1,0:T(8,128)} %get-tuple-element.13.conf_in, f32[32,2,128]{2,1,0:T(2,128)} %get-tuple-element.14.back_in, bf16[192,192]{1,0:T(8,128)(2,1)} %get-tuple-element.15.amat_in, ...), custom_call_target="tpu_custom_call" | custom-call | tf_op jit(solution)/shard_map/pallas_call | solution.py:519

commit v6 on v5

--- a/solution.py
+++ b/solution.py
@@ -24,9 +24,9 @@
 BLOCK = 16
 GROUP = BLOCK // 2
 NBLOCK = SLOTS // BLOCK
-STRESS_AT = 1
+STRESS_AT = 2
 UNROLL = 8
-SHIFTS = (0, 2, 1, 3)
+SHIFTS = (1, 2, 3, 0)
 
 
 def iota(shape, dim):

time: 20.9 us -> 20.8 us (level)
  no operation moved by 1% of the time
where the time goes in v6:
time: 20.8 us; the launch traced here: 20.7 us
  Pallas kernels  20 us (96%)
  between operations  0.64 us (3%)
    pallas_call x1, Pallas kernels, shards(): pl.pallas_call(functools.partial(kernel, *sizes), out_shape=(vel, conf, s...  17.8 us
    pallas_call x1, Pallas kernels, shards(): pl.pallas_call(finish, out_shape=(vel, conf, shape((6, FLAG), F32)), in_s...  2.2 us

profile of v6, /device:TPU:1, one launch (start us, length us, event | category | flops | bytes accessed | tf_op | source)
XLA Modules:
  0.0 20.7 jit_solution(4860085420502984599)
XLA Ops:
  0.6 17.8 %shard_map.85 = (f32[3,192,128]{2,1,0:T(8,128)}, f32[3,64,512]{2,1,0:T(8,128)}, f32[32,2,128]{2,1,0:T(2,128)}, bf16[192,192]{1,0:T(8,128)(2,1)}, f32[32,128]{1,0:T(8,128)}, /*index=5*/s32[1,32]{1,0:T(1,128)}) custom-call(f32[3,192,128]{2,1,0:T(8,128)} %bitcast.6, f32[192,128]{1,0:T(8,128)} %bitcast.7, s32[32]{0:T(128)} %cells_in.1, s32[1,32]{1,0:T(1,128)} %bitcast.8, ...), custom_call_target="tpu_custom_call" | custom-call | tf_op jit(solution)/shard_map/pallas_call | solution.py:503
  18.5 2.2 %shard_map.86 = (f32[3,192,128]{2,1,0:T(8,128)}, f32[3,64,512]{2,1,0:T(8,128)}, f32[6,32]{1,0:T(8,128)}) custom-call(f32[3,192,128]{2,1,0:T(8,128)} %get-tuple-element.12.vel_in, f32[3,64,512]{2,1,0:T(8,128)} %get-tuple-element.13.conf_in, f32[32,2,128]{2,1,0:T(2,128)} %get-tuple-element.14.back_in, bf16[192,192]{1,0:T(8,128)(2,1)} %get-tuple-element.15.amat_in, ...), custom_call_target="tpu_custom_call" | custom-call | tf_op jit(solution)/shard_map/pallas_call | solution.py:519

commit v7 on v5

--- a/solution.py
+++ b/solution.py
@@ -301,14 +301,19 @@
 
     def block_work(order):
         block = block_of(order, 1)
-        arrive(order, block, recv1, r1_sem)
         slots = pl.ds(pl.multiple_of(block * BLOCK, BLOCK), BLOCK)
-        for s in range(GROUP):
-            kst[pl.ds(2 * s, 2), :] = recv1[block * GROUP + s]
-        kappa = kst[...] * 0.01
-        for k in range(9):
-            wide = jnp.broadcast_to(kappa[:, k : k + 1], (BLOCK, 128))
-            kb[k] = wide + 1.0 if k % 4 == 0 else wide
+        if order < 2:
+            ready = range(1) if order == 0 else range(1, NBLOCK)
+            for other in ready:
+                arrive(other, block_of(other, 1), recv1, r1_sem)
+            for other in ready:
+                for s in range(GROUP):
+                    kst[other, pl.ds(2 * s, 2), :] = recv1[block_of(other, 1) * GROUP + s]
+            for other in ready:
+                kappa = kst[other] * 0.01
+                for k in range(9):
+                    wide = jnp.broadcast_to(kappa[:, k : k + 1], (BLOCK, 128))
+                    kb[other, k] = wide + 1.0 if k % 4 == 0 else wide
 
         def step(t, state):
             new = []
@@ -321,8 +326,8 @@
                     here_q = (q0, q1, q2)[a]
                     other = [b for b in range(3) if b != a]
                     new.append(
-                        (kb[4 * a] - pull) * here_q
-                        + (kb[3 * a + other[0]] * (q0, q1, q2)[other[0]] + kb[3 * a + other[1]] * (q0, q1, q2)[other[1]])
+                        (kb[order, 4 * a] - pull) * here_q
+                        + (kb[order, 3 * a + other[0]] * (q0, q1, q2)[other[0]] + kb[order, 3 * a + other[1]] * (q0, q1, q2)[other[1]])
                         + nf[t, a, slots, chunk(c)]
                     )
             return tuple(new)
@@ -486,7 +491,7 @@
         vmem(3, SLOTS, BEADS),
         pltpu.VMEM((STEPS, 3, SLOTS, BEADS), BF16), vmem(STEPS, 3, SLOTS, BEADS),
         vmem(10, FLAG, NZ), vmem(FLAG, NZ), vmem(3, ROWS, NZ),
-        vmem(BLOCK, 128), vmem(9, BLOCK, 128), vmem(BLOCK, 128),
+        vmem(NBLOCK, BLOCK, 128), vmem(NBLOCK, 9, BLOCK, 128), vmem(BLOCK, 128),
         vmem(32, 2, 128), vmem(32, 2, 128), vmem(32, 2, 128),
         vmem(2, 3, NX, NZ), vmem(3, NY, NZ), vmem(2, 3, NY, NZ), vmem(2, 3, NX, NZ), vmem(3, NY, NZ),
         vmem(6, ROWS, NZ),

time: 20.9 us -> 20.9 us (level)
  no operation moved by 1% of the time
where the time goes in v7:
time: 20.9 us; the launch traced here: 20.8 us
  Pallas kernels  20.2 us (97%)
  between operations  0.64 us (3%)
    pallas_call x1, Pallas kernels, shards(): pl.pallas_call(functools.partial(kernel, *sizes), out_shape=(vel, conf, s...  18 us
    pallas_call x1, Pallas kernels, shards(): pl.pallas_call(finish, out_shape=(vel, conf, shape((6, FLAG), F32)), in_s...  2.2 us

profile of v7, /device:TPU:1, one launch (start us, length us, event | category | flops | bytes accessed | tf_op | source)
XLA Modules:
  0.0 20.8 jit_solution(11277795426259443384)
XLA Ops:
  0.6 18.0 %shard_map.85 = (f32[3,192,128]{2,1,0:T(8,128)}, f32[3,64,512]{2,1,0:T(8,128)}, f32[32,2,128]{2,1,0:T(2,128)}, bf16[192,192]{1,0:T(8,128)(2,1)}, f32[32,128]{1,0:T(8,128)}, /*index=5*/s32[1,32]{1,0:T(1,128)}) custom-call(f32[3,192,128]{2,1,0:T(8,128)} %bitcast.6, f32[192,128]{1,0:T(8,128)} %bitcast.7, s32[32]{0:T(128)} %cells_in.1, s32[1,32]{1,0:T(1,128)} %bitcast.8, ...), custom_call_target="tpu_custom_call" | custom-call | tf_op jit(solution)/shard_map/pallas_call | solution.py:508
  18.6 2.2 %shard_map.86 = (f32[3,192,128]{2,1,0:T(8,128)}, f32[3,64,512]{2,1,0:T(8,128)}, f32[6,32]{1,0:T(8,128)}) custom-call(f32[3,192,128]{2,1,0:T(8,128)} %get-tuple-element.12.vel_in, f32[3,64,512]{2,1,0:T(8,128)} %get-tuple-element.13.conf_in, f32[32,2,128]{2,1,0:T(2,128)} %get-tuple-element.14.back_in, bf16[192,192]{1,0:T(8,128)(2,1)} %get-tuple-element.15.amat_in, ...), custom_call_target="tpu_custom_call" | custom-call | tf_op jit(solution)/shard_map/pallas_call | solution.py:524
